TPU v7x, 128 devices: a whole 4x4x4 slice. The times are simulated.
128 devices in a mesh: seq: 64 (over z, y, x), tensor: 2 (over core).
Axes of the slice: x: 4, y: 4, z: 4, core: 2. Of those that a mesh axis runs over, the one named last changes fastest.
Arguments:
- tokens: bfloat16 [8192, 1536], P('seq'), may hold values from -7.5 to 7.5
- attn_weight: bfloat16 [3, 1536, 1536], P(None, None, 'tensor'), may hold values from -2 to 2
- out_weight: bfloat16 [1536, 1536], P('tensor'), may hold values from -0.15625 to 0.15625
- norm_attn: float32 [1536], replicated, may hold values from 0.25 to 1.75
- norm_moe: float32 [1536], replicated, may hold values from 0.25 to 1.75
- routes: int32 [8192, 2], P('seq'), may hold values from 0 to 15, all different within a row; in each aligned block of 128 rows (0 to 127, 128 to 255, ...) at most 24 rows name the same one
- route_weight: float32 [8192, 2], P('seq'), may hold values from 0.1 to 1
- expert_in: bfloat16 [64, 2, 1536, 1536], P('seq', None, None, 'tensor'), may hold values from -0.15625 to 0.15625
- expert_out: bfloat16 [64, 1536, 1536], P('seq', 'tensor'), may hold values from -0.078125 to 0.078125
Outputs:
- layer_out: bfloat16 [8192, 1536], P('seq', 'tensor')
Inputs may be any that keep to these rules, and one draw needn't show every extreme that they name: `routes`: in the rows of one device no expert is named by more than 24 rows, a bound that some block reaches; the two experts of a token differ.
All inputs are finite; a program needn't handle non-finite values.
Results may differ from a plain program's by a relative error of at most 0.017.
The roundings to bfloat16 on the way count: a program that leaves them out, or rounds other values in their place, can miss the bound.
Values may be sent and summed in bfloat16 or wider, within the bound.
A program may use at most 192 MiB of HBM per device.

v0:
```python
import jax
import jax.numpy as jnp
from jax import lax
from jax.sharding import PartitionSpec as P

EXPERTS = 16
HD = 96


eps = 1e-06


def rms_scale(values, gain_row):
    mean_square = jnp.mean(values * values, axis=-1, keepdims=True)
    return values * lax.rsqrt(mean_square + eps) * gain_row


def slot_index(route_rows, expert_count, capacity):
    flat_ids = route_rows.reshape(-1)
    onehot = (flat_ids[:, None] == jnp.arange(expert_count, dtype=jnp.int32)[None, :]).astype(
        jnp.int32
    )
    before = jnp.cumsum(onehot, axis=0) - onehot
    return flat_ids * capacity + jnp.sum(before * onehot, axis=1)


def on_device(
    tokens,
    attn_weight,
    out_weight,
    norm_attn,
    norm_moe,
    routes,
    route_weight,
    expert_in,
    expert_out,
):
    seq_count = lax.axis_size("seq")
    width_count = lax.axis_size("tensor")
    tensor_pos = lax.axis_index("tensor")
    tok_rows, model_width = tokens.shape
    expert_count = EXPERTS
    split_count = seq_count // expert_count
    capacity = 3 * tok_rows // expert_count
    col_width = model_width // width_count
    local_heads = attn_weight.shape[2] // HD
    normed = rms_scale(tokens.astype(jnp.float32), norm_attn).astype(jnp.bfloat16)
    queries = jnp.dot(normed, attn_weight[0], preferred_element_type=jnp.float32).astype(
        jnp.bfloat16
    )
    queries = queries.reshape(tok_rows, local_heads, HD)
    keys_local = jnp.dot(normed, attn_weight[1], preferred_element_type=jnp.float32).astype(
        jnp.bfloat16
    )
    values_local = jnp.dot(normed, attn_weight[2], preferred_element_type=jnp.float32).astype(
        jnp.bfloat16
    )
    row_peak = jnp.full((local_heads, tok_rows), -1e30, jnp.float32)
    key_part = lax.all_gather(keys_local, "seq", axis=0, tiled=True)
    value_part = lax.all_gather(values_local, "seq", axis=0, tiled=True)
    piece_rows = key_part.shape[0]
    key_heads = key_part.reshape(piece_rows, local_heads, HD)
    value_heads = value_part.reshape(piece_rows, local_heads, HD)
    scores = jnp.einsum(
        "qhd,khd->hqk", queries, key_heads, preferred_element_type=jnp.float32
    ) * HD ** (-0.5)
    new_peak = jnp.maximum(row_peak, jnp.max(scores, axis=2))
    exp_scores = jnp.exp(scores - new_peak[:, :, None])
    new_total = jnp.sum(exp_scores, axis=2)
    prob_rows = exp_scores.astype(jnp.bfloat16)
    update = jnp.einsum("hqk,khd->hqd", prob_rows, value_heads, preferred_element_type=jnp.float32)
    heads_out = (update / new_total[:, :, None]).astype(jnp.bfloat16)
    heads_out = heads_out.transpose(1, 0, 2).reshape(tok_rows, local_heads * HD)
    attn_part = jnp.dot(heads_out, out_weight, preferred_element_type=jnp.float32)
    route_index = slot_index(routes, expert_count, capacity)
    attn_cols = lax.psum_scatter(
        attn_part.astype(jnp.bfloat16), "tensor", scatter_dimension=1, tiled=True
    ).astype(jnp.float32)
    token_cols = lax.dynamic_slice_in_dim(tokens, tensor_pos * col_width, col_width, 1)
    hidden_cols = token_cols.astype(jnp.float32) + attn_cols
    square_sum = lax.psum(jnp.sum(hidden_cols * hidden_cols, axis=1), "tensor")
    gain_cols = lax.dynamic_slice_in_dim(norm_moe, tensor_pos * col_width, col_width, 0)
    inverse_rms = lax.rsqrt(square_sum / model_width + eps)
    moe_cols = (hidden_cols * inverse_rms[:, None] * gain_cols).astype(jnp.bfloat16)
    dispatch_rows = jnp.zeros((expert_count * capacity, col_width), jnp.bfloat16)
    dispatch_rows = dispatch_rows.at[route_index].set(jnp.repeat(moe_cols, 2, axis=0))
    dispatch_rows = dispatch_rows.reshape(expert_count, capacity, col_width)
    dispatch_rows = jnp.repeat(dispatch_rows, split_count, axis=0)
    arrived = lax.all_to_all(dispatch_rows, "seq", split_axis=0, concat_axis=0, tiled=True)
    arrived = arrived.reshape(seq_count * capacity, col_width)
    part_rows = lax.all_gather(arrived, "tensor", axis=1, tiled=True)
    weight_rows = expert_in[0]
    gate_sum = jnp.dot(part_rows, weight_rows[0], preferred_element_type=jnp.float32)
    up_sum = jnp.dot(part_rows, weight_rows[1], preferred_element_type=jnp.float32)
    activated = (jax.nn.silu(gate_sum) * up_sum).astype(jnp.bfloat16)
    expert_part = jnp.dot(activated, expert_out[0], preferred_element_type=jnp.float32)
    part_cols = lax.psum_scatter(
        expert_part.astype(jnp.bfloat16), "tensor", scatter_dimension=1, tiled=True
    )
    part_cols = part_cols.reshape(seq_count, capacity, col_width)
    returned = lax.all_to_all(part_cols, "seq", split_axis=0, concat_axis=0, tiled=True)
    returned = returned.reshape(expert_count, split_count, capacity, col_width).astype(jnp.float32)
    expert_cols = jnp.sum(returned, axis=1).astype(jnp.bfloat16)
    expert_cols = expert_cols.reshape(expert_count * capacity, col_width)
    picked = expert_cols[route_index].astype(jnp.float32).reshape(tok_rows, 2, col_width)
    combined = jnp.sum(picked * route_weight[:, :, None], axis=1)
    return (hidden_cols + combined).astype(jnp.bfloat16)


def solution(mesh):
    return jax.shard_map(
        on_device,
        mesh=mesh,
        in_specs=(
            P("seq", None),
            P(None, None, "tensor"),
            P("tensor", None),
            P(),
            P(),
            P("seq", None),
            P("seq", None),
            P("seq", None, None, "tensor"),
            P("seq", "tensor", None),
        ),
        out_specs=P("seq", "tensor"),
        check_vma=False,
    )
```

profile of v0, /device:TPU:0, one launch (start us, length us, event | category | flops | bytes accessed | tf_op | source)
XLA Modules:
  0.0 407.8 jit_solution(6922015783362993903)
XLA Ops:
  6.5 1.3 fusion.41
  7.9 3.0 fusion.29
  10.9 0.0 all-gather.6.cloned.1.call-start
  11.0 3.0 fusion.32
  14.0 0.0 reduce-scatter.3.cloned.1.call-start
  14.1 2.2 fusion.26
  16.3 0.2 copy.14
  16.5 0.1 copy.18
  16.6 0.1 eq.29
  16.7 87.9 %all-gather.4.cloned.1.call-done = bf16[8192,768]{1,0:T(8,128)(2,1)} async-done(((bf16[128,768]{1,0:T(8,128)(2,1)}), bf16[8192,768]{1,0:T(8,128)(2,1)}) %all-gather.4.cloned.1.call-update) | async-done | bytes 12582928 | tf_op jit(solution)/shard_map/all_gather | solution.py:59
  104.6 16.7 %copy.15 = bf16[8192,768]{0,1:T(8,128)(2,1)} copy(bf16[8192,768]{1,0:T(8,128)(2,1)} %all-gather.4.cloned.1.call-done) | data formatting | bytes 25165824 | tf_op jit(solution)/shard_map/all_gather | solution.py:59
  121.3 16.0 %multiply_reduce_fusion = (f32[8,128]{1,0:T(8,128)S(1)}, f32[8,128,8192]{2,1,0:T(8,128)}) fusion(bf16[128,8,96]{0,2,1:T(8,128)(2,1)S(1)} %bitcast.80, bf16[8192,8,96]{0,2,1:T(8,128)(2,1)} %bitcast.72), kind=kOutput, calls=%fused_computation.3 | convolution fusion | flops 1627388928 | bytes 46338048 | tf_op jit(solution)/shard_map/qhd,khd->hqk/dot_general | solution.py:64
  137.3 14.6 %fusion = f32[8,128]{1,0:T(8,128)S(1)} fusion(f32[8,128,8192]{2,1,0:T(8,128)} %get-tuple-element.6, f32[8,128]{1,0:T(8,128)S(1)} %broadcast_maximum_fusion), kind=kLoop, calls=%fused_computation.4 | loop fusion | flops 25164800 | bytes 33562624 | tf_op jit(solution)/shard_map/reduce_sum | solution.py:69
  151.8 46.2 %all-gather.6.cloned.1.call-done = bf16[8192,768]{1,0:T(8,128)(2,1)} async-done(((bf16[128,768]{1,0:T(8,128)(2,1)}), bf16[8192,768]{1,0:T(8,128)(2,1)}) %all-gather.6.cloned.1.call-update) | async-done | bytes 12582928 | tf_op jit(solution)/shard_map/all_gather | solution.py:60
  198.1 16.6 %copy.16 = bf16[8192,768]{0,1:T(8,128)(2,1)} copy(bf16[8192,768]{1,0:T(8,128)(2,1)} %all-gather.6.cloned.1.call-done) | data formatting | bytes 25165824 | tf_op jit(solution)/shard_map/all_gather | solution.py:60
  214.7 16.9 %fusion.38 = bf16[128,8,96]{0,2,1:T(8,128)(2,1)S(1)} fusion(bf16[8192,8,96]{0,2,1:T(8,128)(2,1)} %bitcast.73, f32[8,128,8192]{2,1,0:T(8,128)} %get-tuple-element.6, f32[8,128]{1,0:T(8,128)S(1)} %broadcast_maximum_fusion, f32[128,8]{0,1:T(8,128)S(1)} %bitcast.81), kind=kOutput, calls=%fused_computation.33 | convolution fusion | flops 1635975168 | bytes 46342144 | tf_op jit(solution)/shard_map/hqk,khd->hqd/dot_general | solution.py:71
  231.6 1.2 convolution_convert_fusion.1
  232.9 0.0 all-gather.8.cloned.1.call-start
  232.9 0.1 eq.25
  233.1 0.6 reduce-window.6
  233.7 0.2 slice_reduce_fusion
  233.9 0.1 copy.17
  234.0 0.1 mul.92
  234.2 0.1 dynamic_slice.7
  234.2 0.1 fusion.48
  234.3 8.6 %reduce-scatter.3.cloned.1.call-done = bf16[128,768]{1,0:T(8,128)(2,1)} async-done(((bf16[128,1536]{1,0:T(8,128)(2,1)}), bf16[128,768]{1,0:T(8,128)(2,1)}) %reduce-scatter.3.cloned.1.call-update) | async-done | bytes 196624 | tf_op jit(solution)/shard_map/reduce_scatter | solution.py:76
  242.9 1.1 multiply_reduce_fusion.2
  244.0 2.6 psum.7
  246.5 1.0 multiply_convert_fusion.1
  247.6 0.2 broadcast_in_dim.10
  247.8 0.9 reshape.128
  248.7 2.3 scatter_custom_fusion
  251.0 0.2 broadcast_in_dim.11
  251.1 43.9 %all_to_all.10 = bf16[64,24,768]{2,1,0:T(8,128)(2,1)} all-to-all(bf16[64,24,768]{2,1,0:T(8,128)(2,1)S(1)} %bitcast.76), channel_id=1, replica_groups=mesh['seq'=64,'tensor'=2] {'seq'}, dimensions={0} | all-to-all | bytes 4718592 | tf_op jit(solution)/shard_map/all_to_all | solution.py:89
  295.0 0.0 all-gather.8.cloned.1.call-update
  295.0 0.2 reduce-scatter.5.cloned.1.call-start
  295.3 13.2 %all-gather.8.cloned.1.call-done = bf16[1536,1536]{1,0:T(8,128)(2,1)} async-done(((bf16[1536,768]{1,0:T(8,128)(2,1)}), bf16[1536,1536]{1,0:T(8,128)(2,1)}) %all-gather.8.cloned.1.call-update) | async-done | bytes 4718608 | tf_op jit(solution)/shard_map/all_gather | solution.py:91
  308.5 9.2 %fusion.8 = f32[1536,768]{1,0:T(8,128)} fusion(bf16[1536,1536]{1,0:T(8,128)(2,1)} %all-gather.8.cloned.1.call-done, bf16[1,2,1536,768]{3,2,1,0:T(8,128)(2,1)} %param.16), kind=kOutput, calls=%fused_computation.15 | convolution fusion | flops 3623878656 | bytes 11796480 | tf_op jit(solution)/shard_map/dot_general | solution.py:93
  317.7 13.8 %convolution_convert_fusion = bf16[1536,1536]{1,0:T(8,128)(2,1)} fusion(bf16[1,768,1536]{2,1,0:T(8,128)(2,1)S(1)} %copy-done, f32[1536,768]{1,0:T(8,128)} %fusion.8, bf16[1536,1536]{1,0:T(8,128)(2,1)} %all-gather.8.cloned.1.call-done, bf16[1,2,1536,768]{3,2,1,0:T(8,128)(2,1)} %param.16), kind=kOutput, calls=%fused_computation.9 | convolution fusion | flops 7257194496 | bytes 18874368 | tf_op jit(solution)/shard_map/dot_general | solution.py:96
  331.5 16.8 %reduce-scatter.5.cloned.1.call-done = bf16[1536,768]{1,0:T(8,128)(2,1)} async-done(((bf16[1536,1536]{1,0:T(8,128)(2,1)}), bf16[1536,768]{1,0:T(8,128)(2,1)}) %reduce-scatter.5.cloned.1.call-update) | async-done | bytes 2359312 | tf_op jit(solution)/shard_map/reduce_scatter | solution.py:97
  348.3 10.7 %all-to-all-start.1 = ((bf16[64,24,768]{2,1,0:T(8,128)(2,1)}), bf16[64,24,768]{2,1,0:T(8,128)(2,1)}, u32[]{:S(2)}, u32[]{:S(2)}) async-start(bf16[64,24,768]{2,1,0:T(8,128)(2,1)} %bitcast.77), calls=%async_computation.3 | async-start | bytes 4718592 | tf_op jit(solution)/shard_map/all_to_all | solution.py:101
  359.0 0.7 copy.21
  359.7 32.7 %all-to-all-done.1 = bf16[64,24,768]{2,1,0:T(8,128)(2,1)} async-done(((bf16[64,24,768]{2,1,0:T(8,128)(2,1)}), bf16[64,24,768]{2,1,0:T(8,128)(2,1)}, u32[]{:S(2)}, u32[]{:S(2)}) %all-to-all-start.1) | async-done | bytes 2359328 | tf_op jit(solution)/shard_map/all_to_all | solution.py:101
  392.5 2.0 bitcast_reduce_fusion
  394.5 1.9 gather_fusion
  396.4 1.4 reshape.115
  397.8 1.9 multiply_reduce_fusion.1
  399.6 1.7 add_convert_fusion
  (28 shorter events, 0.2 us)
Async XLA Ops:
  6.5 311.2 %copy-start = (bf16[1,768,1536]{2,1,0:T(8,128)(2,1)S(1)}, bf16[1,768,1536]{2,1,0:T(8,128)(2,1)}, u32[]{:S(2)}) copy-start(bf16[1,768,1536]{2,1,0:T(8,128)(2,1)} %param.17) | copy-start | bytes 7077892
  6.5 7.5 %copy-start.1 = (bf16[128,1536]{1,0:T(8,128)(2,1)S(1)}, bf16[128,1536]{1,0:T(8,128)(2,1)}, u32[]{:S(2)}) copy-start(bf16[128,1536]{1,0:T(8,128)(2,1)} %param.9) | copy-start | bytes 1179652
  6.5 7.5 %copy-start.6 = (f32[1536]{0:T(1024)S(1)}, f32[1536]{0:T(1024)}, u32[]{:S(2)}) copy-start(f32[1536]{0:T(1024)} %param.12) | copy-start | bytes 18436
  6.5 98.1 %all-gather.4.cloned.1.call-start = ((), (), s32[]{:S(2)}) async-start(), calls=%async_computation.4 | async-start | bytes 12779520 | tf_op jit(solution)/shard_map/all_gather | solution.py:59
  10.9 5.6 %copy-start.3 = (s32[128,2]{0,1:T(2,128)S(1)}, s32[128,2]{0,1:T(2,128)}, u32[]{:S(2)}) copy-start(s32[128,2]{0,1:T(2,128)} %param.14) | copy-start | bytes 3076
  10.9 187.1 %all-gather.6.cloned.1.call-start = ((), (), s32[]{:S(2)}) async-start(), calls=%async_computation.5 | async-start | bytes 12779520 | tf_op jit(solution)/shard_map/all_gather | solution.py:60
  14.0 228.9 %reduce-scatter.3.cloned.1.call-start = ((), (), s32[]{:S(2)}) async-start(), calls=%async_computation.6 | async-start | bytes 589824 | tf_op jit(solution)/shard_map/reduce_scatter | solution.py:76
  214.7 16.9 %copy-start.2 = (bf16[768,1536]{1,0:T(8,128)(2,1)S(1)}, bf16[768,1536]{1,0:T(8,128)(2,1)}, u32[]{:S(2)}) copy-start(bf16[768,1536]{1,0:T(8,128)(2,1)} %param.11) | copy-start | bytes 7077892
  214.7 19.5 %copy-start.4 = (f32[1536]{0:T(1024)S(1)}, f32[1536]{0:T(1024)}, u32[]{:S(2)}) copy-start(f32[1536]{0:T(1024)} %param.13) | copy-start | bytes 18436
  232.9 75.7 %all-gather.8.cloned.1.call-start = ((), (), s32[]{:S(2)}) async-start(), calls=%async_computation.7 | async-start | bytes 7077888 | tf_op jit(solution)/shard_map/all_gather | solution.py:91
  295.0 53.3 %reduce-scatter.5.cloned.1.call-start = ((), (), s32[]{:S(2)}) async-start(), calls=%async_computation.8 | async-start | bytes 7077888 | tf_op jit(solution)/shard_map/reduce_scatter | solution.py:97
  331.5 27.5 %copy-start.5 = (f32[128,2]{0,1:T(2,128)S(1)}, f32[128,2]{0,1:T(2,128)}, u32[]{:S(2)}) copy-start(f32[128,2]{0,1:T(2,128)} %param.15) | copy-start | bytes 3076
  348.3 44.2 %all-to-all-start.1 = ((bf16[64,24,768]{2,1,0:T(8,128)(2,1)}), bf16[64,24,768]{2,1,0:T(8,128)(2,1)}, u32[]{:S(2)}, u32[]{:S(2)}) async-start(bf16[64,24,768]{2,1,0:T(8,128)(2,1)} %bitcast.77), calls=%async_computation.3 | async-start | bytes 4718592 | tf_op jit(solution)/shard_map/all_to_all | solution.py:101
Sparse Core Ops, SparseCore 0:
  11.0 93.5 all-gather.3
  107.4 90.6 all-gather.5
  233.0 9.8 reduce-scatter.2
  295.2 13.3 all-gather.7
  331.7 16.5 reduce-scatter.4
where the time goes:
time: 409 us; the launch traced here: 408 us
  waiting for transfers between devices  206 us (50%)
  matrix products  65.3 us (16%)
  blocking collectives  46.5 us (11%)
  local copies, waits for them, and re-layouts  42 us (10%)
  other arithmetic  24.3 us (6%)
  between operations  13.3 us (3%)
  starting transfers between devices  11 us (3%)
    all_gather x1, waiting for transfers between devices, on_device(): key_part = lax.all_gather(keys_local, 'seq', axis=0, tiled=True)  87.9 us
    all_gather x1, waiting for transfers between devices, on_device(): value_part = lax.all_gather(values_local, 'seq', axis=0, tiled=True)  46.2 us
    all_to_all x1, blocking collectives, on_device(): lax.all_to_all(dispatch_rows, 'seq', split_axis=0, concat_axis=0, tiled=T...  43.9 us
    all_to_all x1, waiting for transfers between devices, on_device(): lax.all_to_all(part_cols, 'seq', split_axis=0, concat_axis=0, tiled=True)  32.7 us
    dot_general x1, matrix products, on_device(): jnp.einsum('hqk,khd->hqd', prob_rows, value_heads, preferred_element_type...  16.9 us
    reduce_scatter x1, waiting for transfers between devices, on_device(): lax.psum_scatter(expert_part.astype(jnp.bfloat16), 'tensor', scatter_dime...  16.8 us
    all_gather x1, local copies, waits for them, and re-layouts, on_device(): key_part = lax.all_gather(keys_local, 'seq', axis=0, tiled=True)  16.7 us
    all_gather x1, local copies, waits for them, and re-layouts, on_device(): value_part = lax.all_gather(values_local, 'seq', axis=0, tiled=True)  16.6 us
  transfers between devices with their start and end apart: 6, of which 6 were waited for; matrix products, arithmetic and copies ran while one was open for 13% of the time, Pallas kernels for 0%

commit v1 on v0

v1 whole, which is shorter than its diff:
```python
import math

import jax
import jax.numpy as jnp
from jax import lax
from jax.experimental import pallas as pl
from jax.experimental.pallas import tpu as pltpu
from jax.sharding import PartitionSpec as P

MESH = pl.DeviceIdType.MESH
D = 1536
HALF = 768
QUART = 384
HD = 96
TOK = 128
EXPERTS = 16
CAP = 24
EPS = 1e-6
F32 = jnp.float32
BF16 = jnp.bfloat16
SCALE = HD ** (-0.5) * math.log2(math.e)


def dot(a, b):
    return jnp.dot(a, b, preferred_element_type=F32)


def remote(src, dst, send_sem, recv_sem, device):
    return pltpu.make_async_remote_copy(
        src_ref=src,
        dst_ref=dst,
        send_sem=send_sem,
        recv_sem=recv_sem,
        device_id=device,
        device_id_type=MESH,
    )


def layer_kernel(
    tokens,
    attn_w,
    out_w,
    norm_attn,
    norm_moe,
    routes,
    route_weight,
    expert_in,
    expert_out,
    out,
    w_buf,
    ow_buf,
    wi_buf,
    wd_buf,
    w_sem,
    kv_send,
    q_send,
    q_t,
    kvb,
    q_pad,
    peak,
    acc,
    o_send,
    heads_t,
    proj_send,
    proj_recv,
    moe_half,
    disp,
    xbuf,
    rows_in,
    y_own,
    y_send,
    y_recv,
    parts,
    diag_recv,
    side_recv,
    back,
    ret,
    kv_ss,
    kv_rs,
    q_ss,
    q_rs,
    ring_ss,
    ring_rs,
    twin_ss,
    twin_rs,
    o_ss,
    o_rs,
    proj_sem,
    d_ss,
    d_rs,
    xr_ss,
    xr_rs,
    xt_ss,
    xt_rs,
    y_ss,
    y_rs,
    r_ss,
    r_rs,
    b_ss,
    b_rs,
):
    s = lax.axis_index("seq")
    c = lax.axis_index("tensor")
    x = s % 4
    plane = s // 4
    z = plane // 4
    y = plane % 4
    side = z // 2
    slot = (z % 2) * 4 + y
    left = (s - x + (x + 3) % 4, c)
    right = (s - x + (x + 1) % 4, c)
    twin = (s, 1 - c)

    def mate(i):
        return ((2 * c + i // 4) * 16 + (i % 4) * 4 + x, side)

    def is_me(i):
        return jnp.logical_and(c == side, i == slot)

    def plane_dev(p):
        return (p * 4 + x, c)

    weight_copies = [
        pltpu.make_async_copy(attn_w.at[1], w_buf.at[1], w_sem.at[1]),
        pltpu.make_async_copy(attn_w.at[2], w_buf.at[2], w_sem.at[2]),
        pltpu.make_async_copy(attn_w.at[0], w_buf.at[0], w_sem.at[0]),
        pltpu.make_async_copy(out_w, ow_buf, w_sem.at[3]),
        pltpu.make_async_copy(expert_in.at[0], wi_buf, w_sem.at[4]),
        pltpu.make_async_copy(expert_out.at[0, :, pl.ds(0, HALF)], wd_buf.at[0], w_sem.at[5]),
        pltpu.make_async_copy(expert_out.at[0, :, pl.ds(HALF, HALF)], wd_buf.at[1], w_sem.at[6]),
    ]
    for copy in weight_copies:
        copy.start()

    barrier = pltpu.get_barrier_semaphore()

    def greet(device):
        pl.semaphore_signal(barrier, inc=1, device_id=device, device_id_type=MESH)

    for device in (left, right, twin):
        greet(device)

    @pl.loop(0, 8)
    def _(i):
        @pl.when(jnp.logical_not(is_me(i)))
        def _():
            greet(mate(i))

    @pl.loop(0, 16)
    def _(p):
        @pl.when(p != plane)
        def _():
            greet(plane_dev(p))

    tok = tokens[...].astype(F32)
    mean_square = jnp.mean(tok * tok, axis=1, keepdims=True)
    normed = (tok * lax.rsqrt(mean_square + EPS) * norm_attn[...]).astype(BF16)
    weight_copies[0].wait()
    kv_send[:, 0:HD, :] = dot(normed, w_buf[1]).T.astype(BF16).reshape(8, HD, TOK)
    weight_copies[1].wait()
    kv_send[:, HD : 2 * HD, :] = dot(normed, w_buf[2]).T.astype(BF16).reshape(8, HD, TOK)

    pl.semaphore_wait(barrier, 3 + 15 + 8 - jnp.where(c == side, 1, 0))

    def exchange(i, src, dst, send_sem, recv_sem, start):
        copy = remote(src, dst, send_sem, recv_sem, mate(i))

        @pl.when(jnp.logical_not(is_me(i)))
        def _():
            if start:
                copy.start()
            else:
                copy.wait_send()

        if start:

            @pl.when(is_me(i))
            def _():
                pltpu.make_async_copy(src, dst, recv_sem).start()

    def lanes(i):
        return pl.ds(pl.multiple_of(i * TOK, TOK), TOK)

    def kv_copy(i, start):
        exchange(
            i,
            kv_send.at[i],
            kvb.at[0, pl.ds(0, 2 * HD), lanes(slot)],
            kv_ss.at[i],
            kv_rs.at[slot],
            start,
        )

    def q_copy(i, start):
        exchange(i, q_send.at[i], q_t.at[:, lanes(slot)], q_ss.at[i], q_rs.at[slot], start)

    @pl.loop(0, 8)
    def _(i):
        kv_copy((i + slot) % 8, True)

    weight_copies[2].wait()
    q_send[...] = (dot(normed, w_buf[0]) * SCALE).T.astype(BF16).reshape(8, HD, TOK)

    @pl.loop(0, 8)
    def _(i):
        q_copy((i + slot) % 8, True)

    @pl.loop(0, 8)
    def _(b):
        kvb[b, 2 * HD : 2 * HD + 32, :] = jnp.ones((32, 8 * TOK), BF16)

    peak[...] = jnp.full(peak.shape, -1e30, F32)
    acc[...] = jnp.zeros(acc.shape, F32)
    q_pad[:, HD:] = jnp.zeros((8 * TOK, TOK - HD), BF16)

    expert_ids = lax.broadcasted_iota(jnp.int32, (TOK, EXPERTS), 1)
    hot = [(routes[:, k : k + 1] == expert_ids).astype(F32) for k in range(2)]
    earlier = (
        lax.broadcasted_iota(jnp.int32, (TOK, TOK), 0)
        > lax.broadcasted_iota(jnp.int32, (TOK, TOK), 1)
    ).astype(BF16)
    before = dot(earlier, (hot[0] + hot[1]).astype(BF16))
    place = [
        jnp.sum(before * hot[k], axis=1, keepdims=True)
        + routes[:, k : k + 1].astype(F32) * (2.0 * CAP)
        for k in range(2)
    ]

    def kv_part(dx, dc, h):
        return kvb.at[2 * dx + dc, pl.ds(0, 2 * HD), pl.ds(h * 512, 512)]

    def ring_copy(to, src_dx, dst_dx, h):
        device = right if to == 0 else left
        return remote(
            kv_part(src_dx, 0, h),
            kv_part(dst_dx, 0, h),
            ring_ss.at[dst_dx, h],
            ring_rs.at[dst_dx, h],
            device,
        )

    def twin_copy(dx, h):
        return remote(kv_part(dx, 0, h), kv_part(dx, 1, h), twin_ss.at[dx, h], twin_rs.at[dx, h], twin)

    ring_own = [[ring_copy(0, 0, 3, h), ring_copy(1, 0, 1, h)] for h in range(2)]
    ring_on = [ring_copy(0, 3, 2, 0), ring_copy(1, 1, 2, 1)]
    for h in range(2):

        @pl.loop(4 * h, 4 * h + 4)
        def _(i):
            remote(
                kv_send.at[i],
                kvb.at[0, pl.ds(0, 2 * HD), lanes(i)],
                kv_ss.at[i],
                kv_rs.at[i],
                mate(i),
            ).wait_recv()

        ring_own[h][0].start()
        ring_own[h][1].start()
        twin_copy(0, h).start()

    @pl.loop(0, 8)
    def _(i):
        remote(q_send.at[i], q_t.at[:, lanes(i)], q_ss.at[i], q_rs.at[i], mate(i)).wait_recv()
        rows = pl.ds(pl.multiple_of(i * TOK, TOK), TOK)
        q_pad[rows, 0:HD] = q_t[:, lanes(i)].astype(F32).T.astype(BF16)

    def attend(dx, dc):
        b = 2 * dx + dc

        @pl.loop(0, 4)
        def _(i):
            rows = pl.ds(pl.multiple_of(i * 256, 256), 256)
            scores = dot(q_pad[rows, :], kvb[b, 0:TOK, :])
            old = peak[rows, :]
            new = jnp.maximum(old, jnp.max(scores, axis=1, keepdims=True))
            probs = jnp.exp2(scores - new[:, 0:1]).astype(BF16)
            update = lax.dot_general(
                probs,
                kvb[b, HD : HD + TOK, :],
                (((1,), (1,)), ((), ())),
                preferred_element_type=F32,
            )
            acc[rows, :] = acc[rows, :] * jnp.exp2(old - new) + update
            peak[rows, :] = new

    attend(0, 0)
    twin_copy(0, 0).wait_recv()
    twin_copy(0, 1).wait_recv()
    attend(0, 1)
    for h in range(2):
        ring_own[h][0].wait_recv()
        if h == 0:
            ring_on[0].start()
        twin_copy(3, h).start()
        ring_own[h][1].wait_recv()
        if h == 1:
            ring_on[1].start()
        twin_copy(1, h).start()
    attend(3, 0)
    attend(1, 0)
    for dx in (3, 1):
        twin_copy(dx, 0).wait_recv()
        twin_copy(dx, 1).wait_recv()
        attend(dx, 1)
    for h in range(2):
        ring_on[h].wait_recv()
        twin_copy(2, h).start()
    attend(2, 0)
    twin_copy(2, 0).wait_recv()
    twin_copy(2, 1).wait_recv()
    attend(2, 1)

    def o_copy(i, start):
        exchange(
            i,
            o_send.at[i],
            heads_t.at[pl.ds(pl.multiple_of(slot * HD, HD), HD), :],
            o_ss.at[i],
            o_rs.at[slot],
            start,
        )

    @pl.loop(0, 8)
    def _(i):
        rows = pl.ds(pl.multiple_of(i * TOK, TOK), TOK)
        turned = acc[rows, :].T
        o_send[i] = (turned[0:HD, :] / turned[HD : HD + 1, :]).astype(BF16)
        o_copy(i, True)

    weight_copies[3].wait()

    @pl.loop(0, 8)
    def _(i):
        remote(
            o_send.at[i],
            heads_t.at[pl.ds(pl.multiple_of(i * HD, HD), HD), :],
            o_ss.at[i],
            o_rs.at[i],
            mate(i),
        ).wait_recv()

    heads = heads_t[...].astype(F32).T.astype(BF16)
    proj = dot(heads, ow_buf[...])
    proj_send[...] = proj.astype(BF16)
    proj_copy = remote(proj_send, proj_recv, proj_sem.at[0], proj_sem.at[1], twin)
    proj_copy.start()

    row_ids = lax.broadcasted_iota(jnp.int32, (2 * EXPERTS * CAP, TOK), 0).astype(F32)
    turned = [jnp.broadcast_to(place[k], (TOK, TOK)).T[0:1, :] for k in range(2)]
    low = jnp.logical_or(row_ids == turned[0], row_ids == turned[1])
    high = jnp.logical_or(row_ids == turned[0] + CAP, row_ids == turned[1] + CAP)
    spread = jnp.concatenate([low.astype(F32).astype(BF16), high.astype(F32).astype(BF16)], axis=1)

    proj_copy.wait_recv()
    hidden = tokens[...].astype(F32) + proj + proj_recv[...].astype(F32)
    inverse = lax.rsqrt(jnp.mean(hidden * hidden, axis=1, keepdims=True) + EPS)
    moe = hidden * inverse * norm_moe[...]
    y_own[0, 0:TOK, :] = hidden[:, 0:HALF]
    y_own[1, 0:TOK, :] = hidden[:, HALF:]
    moe_half[2] = y_own[c, 0:TOK, :]
    moe_half[0] = moe[:, 0:HALF]
    moe_half[1] = moe[:, HALF:]
    mine = moe_half[c].astype(BF16)
    stacked = jnp.concatenate([mine[:, 0:QUART], mine[:, QUART:]], axis=0)
    disp[...] = dot(spread, stacked).astype(BF16).reshape(EXPERTS, 2 * CAP, QUART)

    def plane_send(p, src, dst, send_sem, recv_sem):
        @pl.when(p != plane)
        def _():
            remote(src, dst, send_sem, recv_sem, plane_dev(p)).start()

        @pl.when(p == plane)
        def _():
            pltpu.make_async_copy(src, dst, recv_sem).start()

    for a in range(4):

        @pl.loop(0, 4)
        def _(b):
            p = ((z + a) % 4) * 4 + (y + b) % 4
            plane_send(p, disp.at[p], xbuf.at[0, c, plane], d_ss.at[p], d_rs.at[plane])

    def x_part(dx, core, a):
        return xbuf.at[dx, core, pl.ds(((z + 4 - a) % 4) * 4, 4)]

    def x_ring(to, src_dx, dst_dx, a):
        return remote(
            x_part(src_dx, c, a),
            x_part(dst_dx, c, a),
            xr_ss.at[dst_dx, a],
            xr_rs.at[dst_dx, a],
            right if to == 0 else left,
        )

    def x_twin(dx, a, arriving):
        core = 1 - c if arriving else c
        return remote(x_part(dx, core, a), x_part(dx, core, a), xt_ss.at[dx, a], xt_rs.at[dx, a], twin)

    for a in range(4):

        @pl.loop(0, 4)
        def _(b):
            p = ((z + 4 - a) % 4) * 4 + b
            remote(disp.at[p], xbuf.at[0, c, p], d_ss.at[p], d_rs.at[p], plane_dev(p)).wait_recv()

        x_ring(0, 0, 3, a).start()
        x_ring(1, 0, 1, a).start()
        x_twin(0, a, False).start()

    def y_copy(dx):
        return remote(y_send.at[dx], y_recv.at[dx], y_ss.at[dx], y_rs.at[dx], twin)

    def chunk(dx):
        for core in range(2):
            piece = xbuf[dx, core].astype(F32)
            for h in range(2):
                at = core * HALF + h * QUART
                rows_in[:, at : at + QUART] = (
                    piece[:, h * CAP : (h + 1) * CAP, :].reshape(EXPERTS * CAP, QUART).astype(BF16)
                )
        rows = rows_in[...]
        gate = dot(rows, wi_buf[0])
        up = dot(rows, wi_buf[1])
        active = (gate / (1.0 + jnp.exp(-gate)) * up).astype(BF16)
        y_send[dx] = dot(active, wd_buf[1 - c]).astype(BF16)
        y_copy(dx).start()
        y_own[dx] = dot(active, wd_buf[c])

    def settle(dx):
        y_copy(dx).wait_recv()
        total = (y_own[dx] + y_recv[dx].astype(F32)).reshape(EXPERTS, CAP, HALF)
        parts[dx, :, 0:CAP, :] = total[:, :, 0:QUART].astype(BF16)
        parts[dx, :, CAP:, :] = total[:, :, QUART:].astype(BF16)

    for copy in weight_copies[4:]:
        copy.wait()
    for a in range(4):
        x_twin(0, a, True).wait_recv()
    chunk(0)
    for a in range(4):
        x_ring(0, 0, 3, a).wait_recv()
        if a < 2:
            x_ring(0, 3, 2, a).start()
        x_twin(3, a, False).start()
        x_ring(1, 0, 1, a).wait_recv()
        if a >= 2:
            x_ring(1, 1, 2, a).start()
        x_twin(1, a, False).start()
    settle(0)

    def half(h):
        return pl.ds(8 * h, 8)

    def far_copy(h):
        return remote(
            parts.at[2, half(h)], diag_recv.at[h], r_ss.at[h], r_rs.at[h], right if h == 0 else left
        )

    def near_copy(dx, h):
        return remote(
            parts.at[dx, half(h)],
            side_recv.at[dx // 2, half(h)],
            r_ss.at[2 + (dx // 2) * 2 + h],
            r_rs.at[2 + (dx // 2) * 2 + h],
            right if dx == 1 else left,
        )

    for a in range(4):
        x_twin(3, a, True).wait_recv()
    chunk(3)
    for a in range(4):
        x_twin(1, a, True).wait_recv()
    chunk(1)
    settle(3)
    near_copy(3, 0).start()
    settle(1)
    near_copy(1, 1).start()
    for a in range(4):
        x_ring(0 if a < 2 else 1, 0, 2, a).wait_recv()
        x_twin(2, a, False).start()
    for a in range(4):
        x_twin(2, a, True).wait_recv()
    chunk(2)
    settle(2)
    far_copy(0).start()
    far_copy(1).start()
    far_copy(0).wait_recv()
    parts[1, 0:8] = (parts[1, 0:8].astype(F32) + diag_recv[0].astype(F32)).astype(BF16)
    near_copy(1, 0).start()
    far_copy(1).wait_recv()
    parts[3, 8:16] = (parts[3, 8:16].astype(F32) + diag_recv[1].astype(F32)).astype(BF16)
    near_copy(3, 1).start()
    for h in range(2):
        near_copy(1, h).wait_recv()
        near_copy(3, h).wait_recv()
        at = slice(8 * h, 8 * h + 8)
        back[at] = (
            parts[0, at].astype(F32) + side_recv[0, at].astype(F32) + side_recv[1, at].astype(F32)
        ).astype(BF16)

    @pl.loop(0, 16)
    def _(i):
        p = ((z + i // 4) % 4) * 4 + (y + i) % 4
        plane_send(p, back.at[p], ret.at[plane], b_ss.at[p], b_rs.at[plane])

    col_ids = lax.broadcasted_iota(jnp.int32, (TOK, 2 * EXPERTS * CAP), 1).astype(F32)
    picks = jnp.concatenate(
        [
            (col_ids == place[k] + float(h * CAP)).astype(F32).astype(BF16)
            for k in range(2)
            for h in range(2)
        ],
        axis=0,
    )

    @pl.loop(0, 16)
    def _(p):
        remote(back.at[p], ret.at[p], b_ss.at[p], b_rs.at[p], plane_dev(p)).wait_recv()

    picked = dot(picks, ret[...].reshape(2 * EXPERTS * CAP, QUART))
    for h in range(2):
        cols = slice(h * QUART, (h + 1) * QUART)
        first = picked[h * TOK : (h + 1) * TOK]
        second = picked[(2 + h) * TOK : (3 + h) * TOK]
        out[:, cols] = (
            moe_half[2, :, cols] + route_weight[:, 0:1] * first + route_weight[:, 1:2] * second
        ).astype(BF16)

    @pl.loop(0, 8)
    def _(i):
        kv_copy(i, False)
        q_copy(i, False)
        o_copy(i, False)

    for h in range(2):
        ring_own[h][0].wait_send()
        ring_own[h][1].wait_send()
        ring_on[h].wait_send()
        for dx in range(4):
            twin_copy(dx, h).wait_send()
    proj_copy.wait_send()

    @pl.loop(0, 16)
    def _(p):
        @pl.when(p != plane)
        def _():
            remote(disp.at[p], xbuf.at[0, c, plane], d_ss.at[p], d_rs.at[plane], plane_dev(p)).wait_send()
            remote(back.at[p], ret.at[plane], b_ss.at[p], b_rs.at[plane], plane_dev(p)).wait_send()

    for a in range(4):
        x_ring(0, 0, 3, a).wait_send()
        x_ring(1, 0, 1, a).wait_send()
        (x_ring(0, 3, 2, a) if a < 2 else x_ring(1, 1, 2, a)).wait_send()
        for dx in range(4):
            x_twin(dx, a, False).wait_send()
    for dx in range(4):
        y_copy(dx).wait_send()
    for h in range(2):
        far_copy(h).wait_send()
        near_copy(1, h).wait_send()
        near_copy(3, h).wait_send()


def on_device(
    tokens,
    attn_weight,
    out_weight,
    norm_attn,
    norm_moe,
    routes,
    route_weight,
    expert_in,
    expert_out,
):
    vmem = pl.BlockSpec(memory_space=pltpu.VMEM)
    hbm = pl.BlockSpec(memory_space=pl.ANY)
    dma = pltpu.SemaphoreType.DMA
    pairs = (EXPERTS, 2 * CAP, QUART)
    scratch = [
        pltpu.VMEM((3, D, HALF), BF16),
        pltpu.VMEM((HALF, D), BF16),
        pltpu.VMEM((2, D, HALF), BF16),
        pltpu.VMEM((2, HALF, HALF), BF16),
        dma((7,)),
        pltpu.VMEM((8, 2 * HD, TOK), BF16),
        pltpu.VMEM((8, HD, TOK), BF16),
        pltpu.VMEM((HD, 8 * TOK), BF16),
        pltpu.VMEM((8, 2 * HD + 32, 8 * TOK), BF16),
        pltpu.VMEM((8 * TOK, TOK), BF16),
        pltpu.VMEM((8 * TOK, TOK), F32),
        pltpu.VMEM((8 * TOK, TOK), F32),
        pltpu.VMEM((8, HD, TOK), BF16),
        pltpu.VMEM((HALF, TOK), BF16),
        pltpu.VMEM((TOK, D), BF16),
        pltpu.VMEM((TOK, D), BF16),
        pltpu.VMEM((3, TOK, HALF), F32),
        pltpu.VMEM(pairs, BF16),
        pltpu.VMEM((4, 2) + pairs, BF16),
        pltpu.VMEM((EXPERTS * CAP, D), BF16),
        pltpu.VMEM((4, EXPERTS * CAP, HALF), F32),
        pltpu.VMEM((4, EXPERTS * CAP, HALF), BF16),
        pltpu.VMEM((4, EXPERTS * CAP, HALF), BF16),
        pltpu.VMEM((4,) + pairs, BF16),
        pltpu.VMEM((2, 8, 2 * CAP, QUART), BF16),
        pltpu.VMEM((2,) + pairs, BF16),
        pltpu.VMEM(pairs, BF16),
        pltpu.VMEM(pairs, BF16),
        dma((8,)),
        dma((8,)),
        dma((8,)),
        dma((8,)),
        dma((4, 2)),
        dma((4, 2)),
        dma((4, 2)),
        dma((4, 2)),
        dma((8,)),
        dma((8,)),
        dma((2,)),
        dma((16,)),
        dma((16,)),
        dma((4, 4)),
        dma((4, 4)),
        dma((4, 4)),
        dma((4, 4)),
        dma((4,)),
        dma((4,)),
        dma((6,)),
        dma((6,)),
        dma((16,)),
        dma((16,)),
    ]
    return pl.pallas_call(
        layer_kernel,
        out_shape=jax.ShapeDtypeStruct((TOK, HALF), BF16),
        in_specs=[vmem, hbm, hbm, vmem, vmem, vmem, vmem, hbm, hbm],
        out_specs=vmem,
        scratch_shapes=scratch,
        compiler_params=pltpu.CompilerParams(
            collective_id=0, has_side_effects=True, vmem_limit_bytes=60 * 1024 * 1024
        ),
        cost_estimate=pl.CostEstimate(
            flops=30_000_000_000, bytes_accessed=17_000_000, transcendentals=9_000_000
        ),
    )(
        tokens,
        attn_weight,
        out_weight,
        norm_attn.reshape(1, D),
        norm_moe.reshape(1, D),
        routes,
        route_weight,
        expert_in,
        expert_out,
    )


def solution(mesh):
    return jax.shard_map(
        on_device,
        mesh=mesh,
        in_specs=(
            P("seq", None),
            P(None, None, "tensor"),
            P("tensor", None),
            P(),
            P(),
            P("seq", None),
            P("seq", None),
            P("seq", None, None, "tensor"),
            P("seq", "tensor", None),
        ),
        out_specs=P("seq", "tensor"),
        check_vma=False,
    )
```

time: 409 us -> 124 us (0.30)
  waiting for transfers between devices: 206 us -> 0 us
  Pallas kernels: 0 us -> 117 us
  matrix products: 65.3 us -> 0 us
  blocking collectives: 46.5 us -> 0 us
  local copies, waits for them, and re-layouts: 42 us -> 7.02 us
  other arithmetic: 24.3 us -> 0 us
  between operations: 13.3 us -> 0.01 us
  starting transfers between devices: 11 us -> 0 us
    all_gather x3 -> x0, waiting for transfers between devices: 147 us -> none  [the longest x1 87.9 us: on_device(): key_part = lax.all_gather(keys_local, 'seq', axis=0, tiled=True)]
    pallas_call x0 -> x1, Pallas kernels: none -> 117 us  [on_device(): pl.pallas_call(layer_kernel, out_shape=jax.ShapeDtypeStruct((TOK, HALF),...]
    dot_general x8 -> x0, matrix products: 65.3 us -> none  [the longest x1 16.9 us: on_device(): jnp.einsum('hqk,khd->hqd', prob_rows, value_heads, preferred_element_type...]
    all_to_all x1 -> x0, blocking collectives: 43.9 us -> none  [on_device(): lax.all_to_all(dispatch_rows, 'seq', split_axis=0, concat_axis=0, tiled=T...]
    all_gather x2 -> x0, local copies, waits for them, and re-layouts: 33.3 us -> none  [the longest x1 16.7 us: on_device(): key_part = lax.all_gather(keys_local, 'seq', axis=0, tiled=True)]
    all_to_all x1 -> x0, waiting for transfers between devices: 32.7 us -> none  [on_device(): lax.all_to_all(part_cols, 'seq', split_axis=0, concat_axis=0, tiled=True)]
    reduce_scatter x2 -> x0, waiting for transfers between devices: 25.3 us -> none  [the longest x1 16.8 us: on_device(): lax.psum_scatter(expert_part.astype(jnp.bfloat16), 'tensor', scatter_dime...]
    reduce_sum x6 -> x0, other arithmetic: 20.9 us -> none  [the longest x1 14.6 us: on_device(): new_total = jnp.sum(exp_scores, axis=2)]
  transfers between devices with their start and end apart: 6 -> 0, of which waited for: 6 -> 0; matrix products, arithmetic and copies ran while one was open for 13% -> 0% of each run, Pallas kernels for 0% -> 0%
where the time goes in v1:
time: 124 us
  Pallas kernels  117 us (94%)
  local copies, waits for them, and re-layouts  7.02 us (6%)
    pallas_call x1, Pallas kernels, on_device(): pl.pallas_call(layer_kernel, out_shape=jax.ShapeDtypeStruct((TOK, HALF),...  117 us
    unnamed x3, local copies, waits for them, and re-layouts  4.43 us

profile of v1, /device:TPU:0, one launch (start us, length us, event | category | flops | bytes accessed | tf_op | source)
XLA Modules:
  0.0 123.7 jit_solution(893620882046392671)
XLA Ops:
  0.0 1.3 %reshape.6.norm_attn = f32[1,1536]{1,0:T(1,128)} reshape(f32[1536]{0:T(1024)} %param.12) | data formatting | bytes 12288 | tf_op jit(solution)/shard_map/reshape | solution.py:650
  1.3 1.3 %reshape.7.norm_moe = f32[1,1536]{1,0:T(1,128)} reshape(f32[1536]{0:T(1024)} %param.13) | data formatting | bytes 12288 | tf_op jit(solution)/shard_map/reshape | solution.py:651
  2.6 1.4 %copy.10.routes = s32[128,2]{1,0:T(8,128)} copy(s32[128,2]{0,1:T(2,128)} %param.14) | data formatting | bytes 2048 | tf_op args[5]
  4.0 1.4 %copy.11.route_weight = f32[128,2]{1,0:T(8,128)} copy(f32[128,2]{0,1:T(2,128)} %param.15) | data formatting | bytes 2048 | tf_op args[6]
  5.4 116.7 %shard_map.91 = bf16[128,768]{1,0:T(8,128)(2,1)} custom-call(bf16[128,1536]{1,0:T(8,128)(2,1)} %tokens.1, bf16[3,1536,768]{2,1,0:T(8,128)(2,1)} %attn_w.1, bf16[768,1536]{1,0:T(8,128)(2,1)} %out_w.1, f32[1,1536]{1,0:T(1,128)} %reshape.6.norm_attn, f32[1,1536]{1,0:T(1,128)} %reshape.7.norm_moe, s32[128,2]{1,0:T(8,128)} %copy.10.routes, ...), custom_call_target="tpu_custom_call" | custom-call | flops 30000001024 | bytes 17000000 | tf_op jit(solution)/shard_map/pallas_call | solution.py:634
  122.1 1.6 %copy.13 = bf16[128,768]{1,0:T(8,128)(2,1)} copy(bf16[128,768]{1,0:T(8,128)(2,1)} %shard_map.91) | data formatting | bytes 393216

commit v2 on v1

v2 whole, which is shorter than its diff:
```python
import math

import jax
import jax.numpy as jnp
from jax import lax
from jax.experimental import pallas as pl
from jax.experimental.pallas import tpu as pltpu
from jax.sharding import PartitionSpec as P

MESH = pl.DeviceIdType.MESH
D = 1536
HALF = 768
BULK = 512
REST = 256
ORDER = (2, 1, 3, 0)
FAR_FIRST = sorted(
    ((a, b) for a in range(4) for b in range(4)),
    key=lambda o: -(min(o[0], 4 - o[0]) + min(o[1], 4 - o[1])),
)
HD = 96
TOK = 128
EXPERTS = 16
CAP = 24
EPS = 1e-6
F32 = jnp.float32
BF16 = jnp.bfloat16
SCALE = HD ** (-0.5) * math.log2(math.e)


def dot(a, b):
    return jnp.dot(a, b, preferred_element_type=F32)


def remote(src, dst, send_sem, recv_sem, device):
    return pltpu.make_async_remote_copy(
        src_ref=src,
        dst_ref=dst,
        send_sem=send_sem,
        recv_sem=recv_sem,
        device_id=device,
        device_id_type=MESH,
    )


def layer_kernel(
    tokens,
    attn_w,
    out_w,
    norm_attn,
    norm_moe,
    routes,
    route_weight,
    expert_in,
    expert_out,
    out,
    w_buf,
    ow_buf,
    wd_buf,
    w_sem,
    kv_send,
    q_send,
    q_t,
    kvb,
    k_nat,
    peak,
    acc,
    o_send,
    heads_t,
    proj_send,
    proj_recv,
    moe_half,
    info,
    tok_rest,
    disp_bulk,
    disp_wide,
    disp_rest,
    x_bulk,
    x_rest,
    rows_bulk,
    rows_rest,
    sums,
    y_send,
    y_recv,
    parts,
    diag_recv,
    side_recv,
    back,
    ret,
    rest_send,
    rest_recv,
    sum_send,
    sum_recv,
    kv_ss,
    kv_rs,
    q_ss,
    q_rs,
    ring_ss,
    ring_rs,
    twin_ss,
    twin_rs,
    o_ss,
    o_rs,
    proj_sem,
    info_ss,
    info_rs,
    tok_ss,
    tok_rs,
    d_ss,
    d_rs,
    e_ss,
    e_rs,
    xr_ss,
    xr_rs,
    xt_ss,
    xt_rs,
    xe_ss,
    xe_rs,
    y_ss,
    y_rs,
    r_ss,
    r_rs,
    rest_ss,
    rest_rs,
    sum_ss,
    sum_rs,
    b_ss,
    b_rs,
):
    s = lax.axis_index("seq")
    c = lax.axis_index("tensor")
    x = s % 4
    plane = s // 4
    z = plane // 4
    y = plane % 4
    side = z // 2
    slot = (z % 2) * 4 + y
    left = (s - x + (x + 3) % 4, c)
    right = (s - x + (x + 1) % 4, c)
    twin = (s, 1 - c)

    def along(dx):
        return (s - x + (x + dx) % 4, c)

    def mate(i):
        return ((2 * c + i // 4) * 16 + (i % 4) * 4 + x, side)

    def is_me(i):
        return jnp.logical_and(c == side, i == slot)

    def plane_dev(p):
        return (p * 4 + x, c)

    weight_copies = [
        pltpu.make_async_copy(attn_w.at[1], w_buf.at[1], w_sem.at[1]),
        pltpu.make_async_copy(attn_w.at[2], w_buf.at[2], w_sem.at[2]),
        pltpu.make_async_copy(attn_w.at[0], w_buf.at[0], w_sem.at[0]),
        pltpu.make_async_copy(out_w, ow_buf, w_sem.at[3]),
        pltpu.make_async_copy(expert_out.at[0, :, pl.ds(0, HALF)], wd_buf.at[0], w_sem.at[4]),
        pltpu.make_async_copy(expert_out.at[0, :, pl.ds(HALF, HALF)], wd_buf.at[1], w_sem.at[5]),
    ]
    moves = (
        (0, 0, BULK),
        (HALF, BULK, BULK),
        (BULK, 2 * BULK, REST),
        (HALF + BULK, 2 * BULK + REST, REST),
    )
    weight_copies += [
        pltpu.make_async_copy(
            expert_in.at[0, k, pl.ds(start, rows)],
            w_buf.at[1 + k, pl.ds(to, rows)],
            w_sem.at[6 + 4 * k + i],
        )
        for k in range(2)
        for i, (start, to, rows) in enumerate(moves)
    ]
    for copy in weight_copies[:3]:
        copy.start()

    barrier = pltpu.get_barrier_semaphore()

    def greet(device):
        pl.semaphore_signal(barrier, inc=1, device_id=device, device_id_type=MESH)

    for device in (left, right, along(2), twin):
        greet(device)

    @pl.loop(0, 8)
    def _(i):
        @pl.when(jnp.logical_not(is_me(i)))
        def _():
            greet(mate(i))

    @pl.loop(0, 16)
    def _(p):
        @pl.when(p != plane)
        def _():
            greet(plane_dev(p))

    tok = tokens[...].astype(F32)
    mean_square = jnp.mean(tok * tok, axis=1, keepdims=True)
    normed = (tok * lax.rsqrt(mean_square + EPS) * norm_attn[...].reshape(1, D)).astype(BF16)

    def exchange(i, src, dst, send_sem, recv_sem, start):
        copy = remote(src, dst, send_sem, recv_sem, mate(i))

        @pl.when(jnp.logical_not(is_me(i)))
        def _():
            if start:
                copy.start()
            else:
                copy.wait_send()

        if start:

            @pl.when(is_me(i))
            def _():
                pltpu.make_async_copy(src, dst, recv_sem).start()

    def far(a):
        return (z + jnp.where(c == side, 1, 0) + a) % 2

    def lanes(i):
        return pl.ds(pl.multiple_of(i * TOK, TOK), TOK)

    def kv_copy(h, i, start):
        exchange(
            i,
            kv_send.at[h, i],
            kvb.at[0, pl.ds(h * HD, HD), lanes(slot)],
            kv_ss.at[h, i],
            kv_rs.at[h, slot],
            start,
        )

    def q_copy(i, start):
        exchange(i, q_send.at[i], q_t.at[pl.ds(0, HD), lanes(slot)], q_ss.at[i], q_rs.at[slot], start)

    for h in range(2):
        weight_copies[h].wait()
        kv_send[h] = dot(normed, w_buf[1 + h]).T.astype(BF16).reshape(8, HD, TOK)
        if h == 0:
            pl.semaphore_wait(barrier, 4 + 15 + 8 - jnp.where(c == side, 1, 0))

        for b in ORDER:

            @pl.loop(0, 2)
            def _(a):
                kv_copy(h, far(a) * 4 + (y + b) % 4, True)

    weight_copies[2].wait()
    q_send[...] = (dot(normed, w_buf[0]) * SCALE).T.astype(BF16).reshape(8, HD, TOK)
    for b in ORDER:

        @pl.loop(0, 2)
        def _(a):
            q_copy(far(a) * 4 + (y + b) % 4, True)

    for copy in weight_copies[3:]:
        copy.start()

    @pl.loop(0, 8)
    def _(b):
        kvb[b, 2 * HD : 2 * HD + 32, :] = jnp.ones((32, 8 * TOK), BF16)

    peak[...] = jnp.full(peak.shape, -1e30, F32)
    acc[...] = jnp.zeros(acc.shape, F32)
    q_t[HD:, :] = jnp.zeros((TOK - HD, 8 * TOK), BF16)

    expert_ids = lax.broadcasted_iota(jnp.int32, (EXPERTS, TOK), 0)
    hot = [(routes[k : k + 1, :] == expert_ids).astype(F32) for k in range(2)]
    earlier = (
        lax.broadcasted_iota(jnp.int32, (TOK, TOK), 0)
        < lax.broadcasted_iota(jnp.int32, (TOK, TOK), 1)
    ).astype(BF16)
    before = dot((hot[0] + hot[1]).astype(BF16), earlier)
    place = [
        jnp.sum(before * hot[k], axis=0, keepdims=True)
        + routes[k : k + 1, :].astype(F32) * float(CAP)
        for k in range(2)
    ]
    info[0] = jnp.zeros((8, TOK), F32)
    for k in range(2):
        info[0, k : k + 1, :] = place[k]
        info[0, 2 + k : 3 + k, :] = route_weight[k : k + 1, :]

    def to_line(ref, send_sem, recv_sem, dx):
        return remote(
            ref.at[0], ref.at[4 - dx], send_sem.at[dx], recv_sem.at[4 - dx], along(dx)
        )

    for dx in (2, 1, 3):
        to_line(info, info_ss, info_rs, dx).start()

    def kv_part(dx, dc, h):
        return kvb.at[2 * dx + dc, pl.ds(h * HD, HD)]

    def ring_copy(to, src_dx, dst_dx, h):
        device = right if to == 0 else left
        return remote(
            kv_part(src_dx, 0, h),
            kv_part(dst_dx, 0, h),
            ring_ss.at[dst_dx, h],
            ring_rs.at[dst_dx, h],
            device,
        )

    def twin_copy(dx, h):
        return remote(kv_part(dx, 0, h), kv_part(dx, 1, h), twin_ss.at[dx, h], twin_rs.at[dx, h], twin)

    ring_own = [[ring_copy(0, 0, 3, h), ring_copy(1, 0, 1, h)] for h in range(2)]
    ring_on = [ring_copy(0, 3, 2, 0), ring_copy(1, 1, 2, 1)]
    for h in range(2):

        @pl.loop(0, 8)
        def _(i):
            remote(
                kv_send.at[h, i],
                kvb.at[0, pl.ds(h * HD, HD), lanes(i)],
                kv_ss.at[h, i],
                kv_rs.at[h, i],
                mate(i),
            ).wait_recv()

        ring_own[h][0].start()
        ring_own[h][1].start()
        twin_copy(0, h).start()

    @pl.loop(0, 8)
    def _(i):
        remote(
            q_send.at[i], q_t.at[pl.ds(0, HD), lanes(i)], q_ss.at[i], q_rs.at[i], mate(i)
        ).wait_recv()

    def attend(dx, dc):
        b = 2 * dx + dc

        k_nat[...] = kvb[b, 0:TOK, :].astype(F32).T.astype(BF16)
        scores = dot(k_nat[...], q_t[...])
        old = peak[...]
        new = jnp.maximum(old, jnp.max(scores, axis=0, keepdims=True))
        probs = jnp.exp2(scores - new).astype(BF16)
        update = dot(kvb[b, HD : HD + TOK, :], probs)
        acc[...] = acc[...] * jnp.exp2(old - new) + update
        peak[...] = new

    attend(0, 0)
    ring_own[0][0].wait_recv()
    ring_on[0].start()
    twin_copy(3, 0).start()
    ring_own[0][1].wait_recv()
    twin_copy(1, 0).start()
    twin_copy(0, 0).wait_recv()
    twin_copy(0, 1).wait_recv()
    attend(0, 1)
    ring_own[1][1].wait_recv()
    ring_on[1].start()
    twin_copy(1, 1).start()
    ring_own[1][0].wait_recv()
    twin_copy(3, 1).start()
    attend(3, 0)
    attend(1, 0)
    for dx in (3, 1):
        twin_copy(dx, 0).wait_recv()
        twin_copy(dx, 1).wait_recv()
        attend(dx, 1)
    for h in range(2):
        ring_on[h].wait_recv()
        twin_copy(2, h).start()
    attend(2, 0)
    twin_copy(2, 0).wait_recv()
    twin_copy(2, 1).wait_recv()
    attend(2, 1)

    def o_copy(i, start):
        exchange(
            i,
            o_send.at[i],
            heads_t.at[pl.ds(pl.multiple_of(slot * HD, HD), HD), :],
            o_ss.at[i],
            o_rs.at[slot],
            start,
        )

    @pl.loop(0, 8)
    def _(i):
        o_send[i] = (acc[0:HD, lanes(i)] / acc[HD : HD + 1, lanes(i)]).astype(BF16)
        o_copy(i, True)

    weight_copies[3].wait()

    @pl.loop(0, 8)
    def _(i):
        remote(
            o_send.at[i],
            heads_t.at[pl.ds(pl.multiple_of(i * HD, HD), HD), :],
            o_ss.at[i],
            o_rs.at[i],
            mate(i),
        ).wait_recv()

    heads = heads_t[...].astype(F32).T.astype(BF16)
    proj = dot(heads, ow_buf[...])
    proj_send[...] = proj.astype(BF16)
    proj_copy = remote(proj_send, proj_recv, proj_sem.at[0], proj_sem.at[1], twin)
    proj_copy.start()

    def spread(dx):
        ids = lax.broadcasted_iota(jnp.int32, (EXPERTS * CAP, TOK), 0).astype(F32)
        hit = jnp.logical_or(ids == info[dx, 0:1, :], ids == info[dx, 1:2, :])
        return hit.astype(F32).astype(BF16)

    def column(row):
        return jnp.broadcast_to(row, (TOK, TOK)).T[:, 0:1]

    def combine(dx, table):
        ids = lax.broadcasted_iota(jnp.int32, (TOK, EXPERTS * CAP), 1).astype(F32)
        total = None
        for k in range(2):
            picks = (ids == column(info[dx, k : k + 1, :])).astype(F32).astype(BF16)
            term = dot(picks, table) * column(info[dx, 2 + k : 3 + k, :])
            total = term if total is None else total + term
        return total

    for dx in (1, 3, 2):
        to_line(info, info_ss, info_rs, 4 - dx).wait_recv()
    proj_copy.wait_recv()
    hidden = tokens[...].astype(F32) + proj + proj_recv[...].astype(F32)
    inverse = lax.rsqrt(jnp.mean(hidden * hidden, axis=1, keepdims=True) + EPS)
    moe = hidden * inverse * norm_moe[...].reshape(1, D)
    sums[0, 0, 0:TOK, :] = hidden[:, 0:HALF]
    sums[0, 1, 0:TOK, :] = hidden[:, HALF:]
    moe_half[2] = sums[0, c, 0:TOK, :]
    moe_half[0] = moe[:, 0:HALF]
    moe_half[1] = moe[:, HALF:]
    mine = moe_half[c].astype(BF16)

    tok_rest[0] = mine[:, BULK:]
    for dx in (2, 1, 3):
        to_line(tok_rest, tok_ss, tok_rs, dx).start()
    own = spread(0)
    rows = dot(own, mine[:, 0:BULK]).reshape(EXPERTS, CAP, BULK)
    disp_bulk[:, 0:CAP, :] = rows[:, :, 0:REST].astype(BF16)
    disp_bulk[:, CAP:, :] = rows[:, :, REST:].astype(BF16)

    def over_plane(a, b, src, dst, send_sem, recv_sem):
        p = ((z + a) % 4) * 4 + (y + b) % 4
        if a == 0 and b == 0:
            return pltpu.make_async_copy(src.at[p], dst.at[plane], recv_sem.at[plane])
        return remote(src.at[p], dst.at[plane], send_sem.at[p], recv_sem.at[plane], plane_dev(p))

    def bulk_copy(a, b):
        return over_plane(a, b, disp_bulk, x_bulk.at[0, c], d_ss, d_rs)

    def rest_copy(a, b):
        return over_plane(a, b, disp_rest, x_rest.at[c], e_ss, e_rs)

    for a, b in FAR_FIRST:
        bulk_copy(a, b).start()
    disp_wide[:, 0:CAP, :] = dot(own, tok_rest[0]).reshape(EXPERTS, CAP, REST)
    for dx in (1, 3, 2):
        to_line(tok_rest, tok_ss, tok_rs, 4 - dx).wait_recv()
        disp_wide[:, dx * CAP : (dx + 1) * CAP, :] = dot(spread(dx), tok_rest[dx]).reshape(
            EXPERTS, CAP, REST
        )
    disp_rest[...] = disp_wide[...].astype(BF16)
    for a, b in FAR_FIRST:
        rest_copy(a, b).start()

    def group(a):
        return pl.ds(((z + 4 - a) % 4) * 4, 4)

    def x_ring(to, src_dx, dst_dx, a):
        return remote(
            x_bulk.at[src_dx, c, group(a)],
            x_bulk.at[dst_dx, c, group(a)],
            xr_ss.at[dst_dx, a],
            xr_rs.at[dst_dx, a],
            right if to == 0 else left,
        )

    def x_twin(dx, a, arriving):
        part = x_bulk.at[dx, 1 - c if arriving else c, group(a)]
        return remote(part, part, xt_ss.at[dx, a], xt_rs.at[dx, a], twin)

    def rest_twin(a, arriving):
        part = x_rest.at[1 - c if arriving else c, group(a)]
        return remote(part, part, xe_ss.at[a], xe_rs.at[a], twin)

    def wait_group(a, src, dst, send_sem, recv_sem):
        @pl.loop(0, 4)
        def _(b):
            p = ((z + 4 - a) % 4) * 4 + b
            remote(src.at[p], dst.at[p], send_sem.at[p], recv_sem.at[p], plane_dev(p)).wait_recv()

    for a in ORDER:
        wait_group(a, disp_bulk, x_bulk.at[0, c], d_ss, d_rs)
        x_ring(0, 0, 3, a).start()
        x_ring(1, 0, 1, a).start()
        x_twin(0, a, False).start()

    def y_copy(dx):
        return remote(y_send.at[dx], y_recv.at[dx], y_ss.at[dx], y_rs.at[dx], twin)

    def first_part(dx):
        for a in ORDER:
            x_twin(dx, a, True).wait_recv()
        for core in range(2):
            piece = x_bulk[dx, core].astype(F32)
            for h in range(2):
                at = core * BULK + h * REST
                rows_bulk[:, at : at + REST] = (
                    piece[:, h * CAP : (h + 1) * CAP, :].reshape(EXPERTS * CAP, REST).astype(BF16)
                )
        for k in range(2):
            sums[dx, k] = dot(rows_bulk[...], w_buf[1 + k, 0 : 2 * BULK, :])

    def second_part(dx):
        for core in range(2):
            wide = x_rest[core].astype(F32)
            rows_rest[:, core * REST : (core + 1) * REST] = (
                wide[:, dx * CAP : (dx + 1) * CAP, :].reshape(EXPERTS * CAP, REST).astype(BF16)
            )
        rows = rows_rest[...]
        gate = sums[dx, 0] + dot(rows, w_buf[1, 2 * BULK :, :])
        up = sums[dx, 1] + dot(rows, w_buf[2, 2 * BULK :, :])
        active = (gate / (1.0 + jnp.exp(-gate)) * up).astype(BF16)
        y_send[dx] = dot(active, wd_buf[1 - c]).astype(BF16)
        y_copy(dx).start()
        sums[dx, 0] = dot(active, wd_buf[c])

    def settle(dx):
        y_copy(dx).wait_recv()
        total = (sums[dx, 0] + y_recv[dx].astype(F32)).reshape(EXPERTS, CAP, HALF)
        parts[dx, :, 0:CAP, :] = total[:, :, 0:REST].astype(BF16)
        parts[dx, :, CAP:, :] = total[:, :, REST:BULK].astype(BF16)
        pair, at = (0 if dx >= 2 else 1), (0 if dx in (2, 1) else CAP)
        rest_send[pair, :, at : at + CAP, :] = total[:, :, BULK:].astype(BF16)

    for copy in weight_copies[4:]:
        copy.wait()
    first_part(0)
    for i, a in enumerate(ORDER):
        x_ring(0, 0, 3, a).wait_recv()
        if i < 2:
            x_ring(0, 3, 2, a).start()
        x_twin(3, a, False).start()
        x_ring(1, 0, 1, a).wait_recv()
        if i >= 2:
            x_ring(1, 1, 2, a).start()
        x_twin(1, a, False).start()
    first_part(3)
    first_part(1)
    for a in ORDER:
        wait_group(a, disp_rest, x_rest.at[c], e_ss, e_rs)
        rest_twin(a, False).start()
    for i, a in enumerate(ORDER):
        x_ring(0 if i < 2 else 1, 0, 2, a).wait_recv()
        x_twin(2, a, False).start()
    first_part(2)
    for a in ORDER:
        rest_twin(a, True).wait_recv()

    def half(h):
        return pl.ds(8 * h, 8)

    def far_copy(h):
        return remote(
            parts.at[2, half(h)], diag_recv.at[h], r_ss.at[h], r_rs.at[h], right if h == 0 else left
        )

    def near_copy(dx, h):
        return remote(
            parts.at[dx, half(h)],
            side_recv.at[dx // 2, half(h)],
            r_ss.at[2 + (dx // 2) * 2 + h],
            r_rs.at[2 + (dx // 2) * 2 + h],
            right if dx == 1 else left,
        )

    def rest_back(pair, a, b):
        return over_plane(
            a, b, rest_send.at[pair], rest_recv.at[pair], rest_ss.at[pair], rest_rs.at[pair]
        )

    def back_copy(a, b):
        return over_plane(a, b, back, ret, b_ss, b_rs)

    def sum_copy(dx):
        return remote(
            sum_send.at[dx], sum_recv.at[4 - dx], sum_ss.at[dx], sum_rs.at[4 - dx], along(dx)
        )

    second_part(2)
    second_part(3)
    settle(2)
    far_copy(0).start()
    far_copy(1).start()
    settle(3)
    near_copy(3, 0).start()
    for a, b in FAR_FIRST:
        rest_back(0, a, b).start()
    second_part(1)
    second_part(0)
    settle(1)
    near_copy(1, 1).start()
    settle(0)
    for a, b in FAR_FIRST:
        rest_back(1, a, b).start()
    far_copy(0).wait_recv()
    parts[1, 0:8] = (parts[1, 0:8].astype(F32) + diag_recv[0].astype(F32)).astype(BF16)
    near_copy(1, 0).start()
    far_copy(1).wait_recv()
    parts[3, 8:16] = (parts[3, 8:16].astype(F32) + diag_recv[1].astype(F32)).astype(BF16)
    near_copy(3, 1).start()

    def rest_sums(pair):
        @pl.loop(0, 16)
        def _(p):
            remote(
                rest_send.at[pair, p],
                rest_recv.at[pair, p],
                rest_ss.at[pair, p],
                rest_rs.at[pair, p],
                plane_dev(p),
            ).wait_recv()

        both = rest_recv[pair].astype(F32)
        found = []
        for i, dx in enumerate((2, 3) if pair == 0 else (1, 0)):
            table = both[:, i * CAP : (i + 1) * CAP, :].reshape(EXPERTS * CAP, REST).astype(BF16)
            found.append(combine(dx, table))
        return found

    found = rest_sums(0)
    for i, dx in enumerate((2, 3)):
        sum_send[dx] = found[i].astype(BF16)
        sum_copy(dx).start()
    for h in range(2):
        near_copy(1, h).wait_recv()
        near_copy(3, h).wait_recv()
        at = slice(8 * h, 8 * h + 8)
        back[at] = (
            parts[0, at].astype(F32) + side_recv[0, at].astype(F32) + side_recv[1, at].astype(F32)
        ).astype(BF16)
    for a, b in FAR_FIRST:
        back_copy(a, b).start()
    found = rest_sums(1)
    sum_send[1] = found[0].astype(BF16)
    sum_copy(1).start()
    rest = moe_half[2, :, BULK:] + found[1]
    for dx in (2, 1, 3):
        sum_copy(4 - dx).wait_recv()
        rest = rest + sum_recv[dx].astype(F32)
    out[:, BULK:] = rest.astype(BF16)

    @pl.loop(0, 16)
    def _(p):
        remote(back.at[p], ret.at[p], b_ss.at[p], b_rs.at[p], plane_dev(p)).wait_recv()

    both = ret[...].astype(F32)
    for h in range(2):
        cols = slice(h * REST, (h + 1) * REST)
        table = both[:, h * CAP : (h + 1) * CAP, :].reshape(EXPERTS * CAP, REST).astype(BF16)
        out[:, cols] = (moe_half[2, :, cols] + combine(0, table)).astype(BF16)

    @pl.loop(0, 8)
    def _(i):
        kv_copy(0, i, False)
        kv_copy(1, i, False)
        q_copy(i, False)
        o_copy(i, False)

    for h in range(2):
        ring_own[h][0].wait_send()
        ring_own[h][1].wait_send()
        ring_on[h].wait_send()
        for dx in range(4):
            twin_copy(dx, h).wait_send()
    proj_copy.wait_send()

    for a, b in FAR_FIRST[:15]:
        bulk_copy(a, b).wait_send()
        rest_copy(a, b).wait_send()
        rest_back(0, a, b).wait_send()
        rest_back(1, a, b).wait_send()
        back_copy(a, b).wait_send()
    for dx in (1, 2, 3):
        to_line(info, info_ss, info_rs, dx).wait_send()
        to_line(tok_rest, tok_ss, tok_rs, dx).wait_send()
        sum_copy(dx).wait_send()
    for i, a in enumerate(ORDER):
        x_ring(0, 0, 3, a).wait_send()
        x_ring(1, 0, 1, a).wait_send()
        (x_ring(0, 3, 2, a) if i < 2 else x_ring(1, 1, 2, a)).wait_send()
        for dx in range(4):
            x_twin(dx, a, False).wait_send()
        rest_twin(a, False).wait_send()
    for dx in range(4):
        y_copy(dx).wait_send()
    for h in range(2):
        far_copy(h).wait_send()
        near_copy(1, h).wait_send()
        near_copy(3, h).wait_send()


def on_device(
    tokens,
    attn_weight,
    out_weight,
    norm_attn,
    norm_moe,
    routes,
    route_weight,
    expert_in,
    expert_out,
):
    vmem = pl.BlockSpec(memory_space=pltpu.VMEM)
    hbm = pl.BlockSpec(memory_space=pl.ANY)
    dma = pltpu.SemaphoreType.DMA
    pairs = (EXPERTS, 2 * CAP, REST)
    fours = (EXPERTS, 4 * CAP, REST)
    scratch = [
        pltpu.VMEM((3, D, HALF), BF16),
        pltpu.VMEM((HALF, D), BF16),
        pltpu.VMEM((2, HALF, HALF), BF16),
        dma((14,)),
        pltpu.VMEM((2, 8, HD, TOK), BF16),
        pltpu.VMEM((8, HD, TOK), BF16),
        pltpu.VMEM((TOK, 8 * TOK), BF16),
        pltpu.VMEM((8, 2 * HD + 32, 8 * TOK), BF16),
        pltpu.VMEM((8 * TOK, TOK), BF16),
        pltpu.VMEM((1, 8 * TOK), F32),
        pltpu.VMEM((TOK, 8 * TOK), F32),
        pltpu.VMEM((8, HD, TOK), BF16),
        pltpu.VMEM((HALF, TOK), BF16),
        pltpu.VMEM((TOK, D), BF16),
        pltpu.VMEM((TOK, D), BF16),
        pltpu.VMEM((3, TOK, HALF), F32),
        pltpu.VMEM((4, 8, TOK), F32),
        pltpu.VMEM((4, TOK, REST), BF16),
        pltpu.VMEM(pairs, BF16),
        pltpu.VMEM(fours, F32),
        pltpu.VMEM(fours, BF16),
        pltpu.VMEM((4, 2) + pairs, BF16),
        pltpu.VMEM((2,) + fours, BF16),
        pltpu.VMEM((EXPERTS * CAP, 2 * BULK), BF16),
        pltpu.VMEM((EXPERTS * CAP, 2 * REST), BF16),
        pltpu.VMEM((4, 2, EXPERTS * CAP, HALF), F32),
        pltpu.VMEM((4, EXPERTS * CAP, HALF), BF16),
        pltpu.VMEM((4, EXPERTS * CAP, HALF), BF16),
        pltpu.VMEM((4,) + pairs, BF16),
        pltpu.VMEM((2, 8, 2 * CAP, REST), BF16),
        pltpu.VMEM((2,) + pairs, BF16),
        pltpu.VMEM(pairs, BF16),
        pltpu.VMEM(pairs, BF16),
        pltpu.VMEM((2,) + pairs, BF16),
        pltpu.VMEM((2,) + pairs, BF16),
        pltpu.VMEM((4, TOK, REST), BF16),
        pltpu.VMEM((4, TOK, REST), BF16),
        dma((2, 8)),
        dma((2, 8)),
        dma((8,)),
        dma((8,)),
        dma((4, 2)),
        dma((4, 2)),
        dma((4, 2)),
        dma((4, 2)),
        dma((8,)),
        dma((8,)),
        dma((2,)),
        dma((4,)),
        dma((4,)),
        dma((4,)),
        dma((4,)),
        dma((16,)),
        dma((16,)),
        dma((16,)),
        dma((16,)),
        dma((4, 4)),
        dma((4, 4)),
        dma((4, 4)),
        dma((4, 4)),
        dma((4,)),
        dma((4,)),
        dma((4,)),
        dma((4,)),
        dma((6,)),
        dma((6,)),
        dma((2, 16)),
        dma((2, 16)),
        dma((4,)),
        dma((4,)),
        dma((16,)),
        dma((16,)),
    ]
    return pl.pallas_call(
        layer_kernel,
        out_shape=jax.ShapeDtypeStruct((TOK, HALF), BF16),
        in_specs=[vmem, hbm, hbm, vmem, vmem, vmem, vmem, hbm, hbm],
        out_specs=vmem,
        scratch_shapes=scratch,
        compiler_params=pltpu.CompilerParams(
            collective_id=0, has_side_effects=True, vmem_limit_bytes=60 * 1024 * 1024
        ),
        cost_estimate=pl.CostEstimate(
            flops=30_000_000_000, bytes_accessed=17_000_000, transcendentals=9_000_000
        ),
    )(
        tokens,
        attn_weight,
        out_weight,
        norm_attn,
        norm_moe,
        routes.T,
        route_weight.T,
        expert_in,
        expert_out,
    )


def solution(mesh):
    return jax.shard_map(
        on_device,
        mesh=mesh,
        in_specs=(
            P("seq", None),
            P(None, None, "tensor"),
            P("tensor", None),
            P(),
            P(),
            P("seq", None),
            P("seq", None),
            P("seq", None, None, "tensor"),
            P("seq", "tensor", None),
        ),
        out_specs=P("seq", "tensor"),
        check_vma=False,
    )
```

time: 124 us -> 103 us (0.83)
  Pallas kernels: 117 us -> 101 us
  local copies, waits for them, and re-layouts: 7.02 us -> 1.62 us
    pallas_call x1, Pallas kernels: 117 us -> 101 us  [on_device(): pl.pallas_call(layer_kernel, out_shape=jax.ShapeDtypeStruct((TOK, HALF),...]
    unnamed x3 -> x1, local copies, waits for them, and re-layouts: 4.43 us -> 1.62 us
    reshape x2 -> x0, local copies, waits for them, and re-layouts: 2.59 us -> none  [the longest x1 1.3 us: on_device(): norm_moe.reshape(1, D)]
where the time goes in v2:
time: 103 us
  Pallas kernels  101 us (98%)
  local copies, waits for them, and re-layouts  1.62 us (2%)
    pallas_call x1, Pallas kernels, on_device(): pl.pallas_call(layer_kernel, out_shape=jax.ShapeDtypeStruct((TOK, HALF),...  101 us

profile of v2, /device:TPU:0, one launch (start us, length us, event | category | flops | bytes accessed | tf_op | source)
XLA Modules:
  0.0 102.9 jit_solution(7369562476839994052)
XLA Ops:
  0.0 101.3 %shard_map.91 = bf16[128,768]{1,0:T(8,128)(2,1)} custom-call(bf16[128,1536]{1,0:T(8,128)(2,1)} %tokens.1, bf16[3,1536,768]{2,1,0:T(8,128)(2,1)} %attn_w.1, bf16[768,1536]{1,0:T(8,128)(2,1)} %out_w.1, f32[1536]{0:T(1024)} %norm_attn.1, f32[1536]{0:T(1024)} %norm_moe.1, s32[2,128]{1,0:T(2,128)} %bitcast.2, f32[2,128]{1,0:T(2,128)} %bitcast.3, ...), custom_call_target="tpu_custom_call" | custom-call | flops 30000001024 | bytes 17000000 | tf_op jit(solution)/shard_map/pallas_call | solution.py:796
  101.3 1.6 %copy.11 = bf16[128,768]{1,0:T(8,128)(2,1)} copy(bf16[128,768]{1,0:T(8,128)(2,1)} %shard_map.91) | data formatting | bytes 393216

commit v3 on v2

--- a/solution.py
+++ b/solution.py
@@ -13,10 +13,7 @@
 BULK = 512
 REST = 256
 ORDER = (2, 1, 3, 0)
-FAR_FIRST = sorted(
-    ((a, b) for a in range(4) for b in range(4)),
-    key=lambda o: -(min(o[0], 4 - o[0]) + min(o[1], 4 - o[1])),
-)
+GROUPS = (0, 1, 3, 2)
 HD = 96
 TOK = 128
 EXPERTS = 16
@@ -43,25 +40,32 @@
 
 
 def layer_kernel(
-    tokens,
+    tokens_in,
     attn_w,
     out_w,
+    norm_attn_in,
+    norm_moe_in,
+    routes_in,
+    route_weight_in,
+    expert_in,
+    expert_out,
+    out,
+    tokens,
     norm_attn,
     norm_moe,
     routes,
     route_weight,
-    expert_in,
-    expert_out,
-    out,
+    small_sem,
     w_buf,
     ow_buf,
     wd_buf,
     w_sem,
+    normed_buf,
     kv_send,
-    q_send,
     q_t,
     kvb,
-    k_nat,
+    score_buf,
+    top,
     peak,
     acc,
     o_send,
@@ -70,6 +74,9 @@
     proj_recv,
     moe_half,
     info,
+    spread,
+    picks,
+    shares,
     tok_rest,
     disp_bulk,
     disp_wide,
@@ -150,6 +157,41 @@
     def plane_dev(p):
         return (p * 4 + x, c)
 
+    barrier = pltpu.get_barrier_semaphore()
+
+    def greet(device):
+        pl.semaphore_signal(barrier, inc=1, device_id=device, device_id_type=MESH)
+
+    for device in (left, right, along(2), twin):
+        greet(device)
+
+    @pl.loop(0, 8)
+    def _(i):
+        @pl.when(jnp.logical_not(is_me(i)))
+        def _():
+            greet(mate(i))
+
+    @pl.loop(0, 16)
+    def _(p):
+        @pl.when(p != plane)
+        def _():
+            greet(plane_dev(p))
+
+    small = [
+        pltpu.make_async_copy(src, dst, small_sem.at[i])
+        for i, (src, dst) in enumerate(
+            (
+                (tokens_in, tokens),
+                (norm_attn_in, norm_attn),
+                (routes_in, routes),
+                (route_weight_in, route_weight),
+                (norm_moe_in, norm_moe),
+            )
+        )
+    ]
+    for copy in small:
+        copy.start()
+
     weight_copies = [
         pltpu.make_async_copy(attn_w.at[1], w_buf.at[1], w_sem.at[1]),
         pltpu.make_async_copy(attn_w.at[2], w_buf.at[2], w_sem.at[2]),
@@ -176,29 +218,11 @@
     for copy in weight_copies[:3]:
         copy.start()
 
-    barrier = pltpu.get_barrier_semaphore()
-
-    def greet(device):
-        pl.semaphore_signal(barrier, inc=1, device_id=device, device_id_type=MESH)
-
-    for device in (left, right, along(2), twin):
-        greet(device)
-
-    @pl.loop(0, 8)
-    def _(i):
-        @pl.when(jnp.logical_not(is_me(i)))
-        def _():
-            greet(mate(i))
-
-    @pl.loop(0, 16)
-    def _(p):
-        @pl.when(p != plane)
-        def _():
-            greet(plane_dev(p))
-
+    small[0].wait()
+    small[1].wait()
     tok = tokens[...].astype(F32)
     mean_square = jnp.mean(tok * tok, axis=1, keepdims=True)
-    normed = (tok * lax.rsqrt(mean_square + EPS) * norm_attn[...].reshape(1, D)).astype(BF16)
+    normed_buf[...] = (tok * lax.rsqrt(mean_square + EPS) * norm_attn[...].reshape(1, D)).astype(BF16)
 
     def exchange(i, src, dst, send_sem, recv_sem, start):
         copy = remote(src, dst, send_sem, recv_sem, mate(i))
@@ -233,27 +257,14 @@
         )
 
     def q_copy(i, start):
-        exchange(i, q_send.at[i], q_t.at[pl.ds(0, HD), lanes(slot)], q_ss.at[i], q_rs.at[slot], start)
-
-    for h in range(2):
-        weight_copies[h].wait()
-        kv_send[h] = dot(normed, w_buf[1 + h]).T.astype(BF16).reshape(8, HD, TOK)
-        if h == 0:
-            pl.semaphore_wait(barrier, 4 + 15 + 8 - jnp.where(c == side, 1, 0))
-
-        for b in ORDER:
-
-            @pl.loop(0, 2)
-            def _(a):
-                kv_copy(h, far(a) * 4 + (y + b) % 4, True)
-
-    weight_copies[2].wait()
-    q_send[...] = (dot(normed, w_buf[0]) * SCALE).T.astype(BF16).reshape(8, HD, TOK)
-    for b in ORDER:
-
-        @pl.loop(0, 2)
-        def _(a):
-            q_copy(far(a) * 4 + (y + b) % 4, True)
+        exchange(i, kv_send.at[2, i], q_t.at[:, lanes(slot)], q_ss.at[i], q_rs.at[slot], start)
+
+    @pl.loop(0, 3)
+    def _(h):
+        at = (h + 1) % 3
+        pltpu.make_async_copy(attn_w.at[at], w_buf.at[at], w_sem.at[at]).wait()
+        scale = jnp.where(h == 2, SCALE, 1.0)
+        kv_send[h] = (dot(normed_buf[...], w_buf[at]) * scale).T.astype(BF16).reshape(8, HD, TOK)
 
     for copy in weight_copies[3:]:
         copy.start()
@@ -264,8 +275,9 @@
 
     peak[...] = jnp.full(peak.shape, -1e30, F32)
     acc[...] = jnp.zeros(acc.shape, F32)
-    q_t[HD:, :] = jnp.zeros((TOK - HD, 8 * TOK), BF16)
-
+
+    for copy in small[2:]:
+        copy.wait()
     expert_ids = lax.broadcasted_iota(jnp.int32, (EXPERTS, TOK), 0)
     hot = [(routes[k : k + 1, :] == expert_ids).astype(F32) for k in range(2)]
     earlier = (
@@ -283,6 +295,15 @@
         info[0, k : k + 1, :] = place[k]
         info[0, 2 + k : 3 + k, :] = route_weight[k : k + 1, :]
 
+    pl.semaphore_wait(barrier, 4 + 15 + 8 - jnp.where(c == side, 1, 0))
+    @pl.loop(0, 16)
+    def _(i):
+        kv_copy(i // 8, far(i) * 4 + (y + 2 + 3 * (i // 2)) % 4, True)
+
+    @pl.loop(0, 8)
+    def _(i):
+        q_copy(far(i) * 4 + (y + 2 + 3 * (i // 2)) % 4, True)
+
     def to_line(ref, send_sem, recv_sem, dx):
         return remote(
             ref.at[0], ref.at[4 - dx], send_sem.at[dx], recv_sem.at[4 - dx], along(dx)
@@ -328,48 +349,92 @@
     @pl.loop(0, 8)
     def _(i):
         remote(
-            q_send.at[i], q_t.at[pl.ds(0, HD), lanes(i)], q_ss.at[i], q_rs.at[i], mate(i)
+            kv_send.at[2, i], q_t.at[:, lanes(i)], q_ss.at[i], q_rs.at[i], mate(i)
         ).wait_recv()
 
-    def attend(dx, dc):
-        b = 2 * dx + dc
-
-        k_nat[...] = kvb[b, 0:TOK, :].astype(F32).T.astype(BF16)
-        scores = dot(k_nat[...], q_t[...])
+    def block(step):
+        dc = jnp.where(step < 2, step, jnp.where(step < 6, step // 4, step - 6))
+        dx = jnp.where(step < 2, 0, jnp.where(step < 6, 3 - 2 * (step % 2), 2))
+        return 2 * dx + dc
+
+    def scores_of(b, at):
+        return dot(kvb[b, 0:HD, at : at + 256].astype(F32).T.astype(BF16), q_t[...])
+
+    def attend(this, following):
         old = peak[...]
-        new = jnp.maximum(old, jnp.max(scores, axis=0, keepdims=True))
-        probs = jnp.exp2(scores - new).astype(BF16)
-        update = dot(kvb[b, HD : HD + TOK, :], probs)
-        acc[...] = acc[...] * jnp.exp2(old - new) + update
+        new = jnp.maximum(old, top[...])
+        update = acc[...] * jnp.exp2(old - new)
+        highest = None
+        for at in range(0, 8 * TOK, 256):
+            if following is not None:
+                scores = scores_of(following, at)
+                here = jnp.max(scores, axis=0, keepdims=True)
+                highest = here if highest is None else jnp.maximum(highest, here)
+            probs = jnp.exp2(score_buf[at : at + 256, :] - new).astype(BF16)
+            update = update + dot(kvb[this, HD : HD + TOK, at : at + 256], probs)
+            if following is not None:
+                score_buf[at : at + 256, :] = scores
+        acc[...] = update
         peak[...] = new
-
-    attend(0, 0)
-    ring_own[0][0].wait_recv()
-    ring_on[0].start()
-    twin_copy(3, 0).start()
-    ring_own[0][1].wait_recv()
-    twin_copy(1, 0).start()
-    twin_copy(0, 0).wait_recv()
-    twin_copy(0, 1).wait_recv()
-    attend(0, 1)
-    ring_own[1][1].wait_recv()
-    ring_on[1].start()
-    twin_copy(1, 1).start()
-    ring_own[1][0].wait_recv()
-    twin_copy(3, 1).start()
-    attend(3, 0)
-    attend(1, 0)
-    for dx in (3, 1):
-        twin_copy(dx, 0).wait_recv()
-        twin_copy(dx, 1).wait_recv()
-        attend(dx, 1)
-    for h in range(2):
-        ring_on[h].wait_recv()
-        twin_copy(2, h).start()
-    attend(2, 0)
-    twin_copy(2, 0).wait_recv()
+        if following is not None:
+            top[...] = highest
+
+    highest = None
+    for at in range(0, 8 * TOK, 256):
+        scores = scores_of(0, at)
+        here = jnp.max(scores, axis=0, keepdims=True)
+        highest = here if highest is None else jnp.maximum(highest, here)
+        score_buf[at : at + 256, :] = scores
+    top[...] = highest
+
+    @pl.loop(1, 8)
+    def _(step):
+        @pl.when(step == 1)
+        def _():
+            twin_copy(0, 0).wait_recv()
+
+        @pl.when(step == 2)
+        def _():
+            ring_own[0][0].wait_recv()
+            ring_on[0].start()
+            twin_copy(3, 0).start()
+            ring_own[0][1].wait_recv()
+            twin_copy(1, 0).start()
+            twin_copy(0, 1).wait_recv()
+
+        @pl.when(step == 3)
+        def _():
+            ring_own[1][1].wait_recv()
+            ring_on[1].start()
+            twin_copy(1, 1).start()
+            ring_own[1][0].wait_recv()
+            twin_copy(3, 1).start()
+
+        @pl.when(step == 4)
+        def _():
+            twin_copy(3, 0).wait_recv()
+
+        @pl.when(step == 5)
+        def _():
+            twin_copy(1, 0).wait_recv()
+            twin_copy(3, 1).wait_recv()
+
+        @pl.when(step == 6)
+        def _():
+            ring_on[0].wait_recv()
+            twin_copy(2, 0).start()
+            twin_copy(1, 1).wait_recv()
+
+        @pl.when(step == 7)
+        def _():
+            ring_on[1].wait_recv()
+            twin_copy(2, 1).start()
+            twin_copy(2, 0).wait_recv()
+
+        attend(block(step - 1), block(step))
+
     twin_copy(2, 1).wait_recv()
-    attend(2, 1)
+    attend(5, None)
 
     def o_copy(i, start):
         exchange(
@@ -404,25 +469,29 @@
     proj_copy = remote(proj_send, proj_recv, proj_sem.at[0], proj_sem.at[1], twin)
     proj_copy.start()
 
-    def spread(dx):
+    def column(row):
+        return jnp.broadcast_to(row, (TOK, TOK)).T
+
+    def fill_spread(dx):
         ids = lax.broadcasted_iota(jnp.int32, (EXPERTS * CAP, TOK), 0).astype(F32)
         hit = jnp.logical_or(ids == info[dx, 0:1, :], ids == info[dx, 1:2, :])
-        return hit.astype(F32).astype(BF16)
-
-    def column(row):
-        return jnp.broadcast_to(row, (TOK, TOK)).T[:, 0:1]
+        spread[dx] = hit.astype(F32).astype(BF16)
+
+    def fill_picks(dx):
+        ids = lax.broadcasted_iota(jnp.int32, (TOK, EXPERTS * CAP), 1).astype(F32)
+        for k in range(2):
+            hit = ids == column(info[dx, k : k + 1, :])[:, 0:1]
+            picks[dx, k * TOK : (k + 1) * TOK, :] = hit.astype(F32).astype(BF16)
+            shares[dx, k] = column(info[dx, 2 + k : 3 + k, :])
 
     def combine(dx, table):
-        ids = lax.broadcasted_iota(jnp.int32, (TOK, EXPERTS * CAP), 1).astype(F32)
-        total = None
-        for k in range(2):
-            picks = (ids == column(info[dx, k : k + 1, :])).astype(F32).astype(BF16)
-            term = dot(picks, table) * column(info[dx, 2 + k : 3 + k, :])
-            total = term if total is None else total + term
-        return total
+        rows = dot(picks[dx], table)
+        return rows[0:TOK] * shares[dx, 0, :, 0:1] + rows[TOK:] * shares[dx, 1, :, 0:1]
 
     for dx in (1, 3, 2):
         to_line(info, info_ss, info_rs, 4 - dx).wait_recv()
+    for dx in range(4):
+        fill_spread(dx)
     proj_copy.wait_recv()
     hidden = tokens[...].astype(F32) + proj + proj_recv[...].astype(F32)
     inverse = lax.rsqrt(jnp.mean(hidden * hidden, axis=1, keepdims=True) + EPS)
@@ -437,34 +506,36 @@
     tok_rest[0] = mine[:, BULK:]
     for dx in (2, 1, 3):
         to_line(tok_rest, tok_ss, tok_rs, dx).start()
-    own = spread(0)
-    rows = dot(own, mine[:, 0:BULK]).reshape(EXPERTS, CAP, BULK)
+    rows = dot(spread[0], mine[:, 0:BULK]).reshape(EXPERTS, CAP, BULK)
     disp_bulk[:, 0:CAP, :] = rows[:, :, 0:REST].astype(BF16)
     disp_bulk[:, CAP:, :] = rows[:, :, REST:].astype(BF16)
 
-    def over_plane(a, b, src, dst, send_sem, recv_sem):
-        p = ((z + a) % 4) * 4 + (y + b) % 4
-        if a == 0 and b == 0:
-            return pltpu.make_async_copy(src.at[p], dst.at[plane], recv_sem.at[plane])
-        return remote(src.at[p], dst.at[plane], send_sem.at[p], recv_sem.at[plane], plane_dev(p))
-
-    def bulk_copy(a, b):
-        return over_plane(a, b, disp_bulk, x_bulk.at[0, c], d_ss, d_rs)
-
-    def rest_copy(a, b):
-        return over_plane(a, b, disp_rest, x_rest.at[c], e_ss, e_rs)
-
-    for a, b in FAR_FIRST:
-        bulk_copy(a, b).start()
-    disp_wide[:, 0:CAP, :] = dot(own, tok_rest[0]).reshape(EXPERTS, CAP, REST)
-    for dx in (1, 3, 2):
-        to_line(tok_rest, tok_ss, tok_rs, 4 - dx).wait_recv()
-        disp_wide[:, dx * CAP : (dx + 1) * CAP, :] = dot(spread(dx), tok_rest[dx]).reshape(
-            EXPERTS, CAP, REST
-        )
-    disp_rest[...] = disp_wide[...].astype(BF16)
-    for a, b in FAR_FIRST:
-        rest_copy(a, b).start()
+    def over_plane(src, dst, send_sem, recv_sem, near=False):
+        @pl.loop(0, 16)
+        def _(i):
+            turn = i // 4
+            if near:
+                a = jnp.where(turn == 2, 3, jnp.where(turn == 3, 2, turn))
+            else:
+                a = (2 + 3 * turn) % 4
+            p = ((z + a) % 4) * 4 + (y + 2 + 3 * i) % 4
+
+            @pl.when(p == plane)
+            def _():
+                pltpu.make_async_copy(src.at[p], dst.at[plane], recv_sem.at[plane]).start()
+
+            @pl.when(p != plane)
+            def _():
+                remote(
+                    src.at[p], dst.at[plane], send_sem.at[p], recv_sem.at[plane], plane_dev(p)
+                ).start()
+
+    def plane_gone(src, dst, send_sem, recv_sem, p):
+        remote(src.at[p], dst.at[plane], send_sem.at[p], recv_sem.at[plane], plane_dev(p)).wait_send()
+
+    bulk_way = (disp_bulk, x_bulk.at[0, c], d_ss, d_rs)
+    rest_way = (disp_rest, x_rest.at[c], e_ss, e_rs)
+    over_plane(*bulk_way, near=True)
 
     def group(a):
         return pl.ds(((z + 4 - a) % 4) * 4, 4)
@@ -492,18 +563,31 @@
             p = ((z + 4 - a) % 4) * 4 + b
             remote(src.at[p], dst.at[p], send_sem.at[p], recv_sem.at[p], plane_dev(p)).wait_recv()
 
-    for a in ORDER:
-        wait_group(a, disp_bulk, x_bulk.at[0, c], d_ss, d_rs)
+    def ring_group(a):
+        wait_group(a, *bulk_way)
         x_ring(0, 0, 3, a).start()
         x_ring(1, 0, 1, a).start()
         x_twin(0, a, False).start()
 
+    ring_group(GROUPS[0])
+    disp_wide[:, 0:CAP, :] = dot(spread[0], tok_rest[0]).reshape(EXPERTS, CAP, REST)
+    for dx in (1, 3, 2):
+        to_line(tok_rest, tok_ss, tok_rs, 4 - dx).wait_recv()
+        disp_wide[:, dx * CAP : (dx + 1) * CAP, :] = dot(spread[dx], tok_rest[dx]).reshape(
+            EXPERTS, CAP, REST
+        )
+    disp_rest[...] = disp_wide[...].astype(BF16)
+    over_plane(*rest_way)
+
+    for a in GROUPS[1:]:
+        ring_group(a)
+    for dx in range(4):
+        fill_picks(dx)
+
     def y_copy(dx):
         return remote(y_send.at[dx], y_recv.at[dx], y_ss.at[dx], y_rs.at[dx], twin)
 
     def first_part(dx):
-        for a in ORDER:
-            x_twin(dx, a, True).wait_recv()
         for core in range(2):
             piece = x_bulk[dx, core].astype(F32)
             for h in range(2):
@@ -515,12 +599,7 @@
             sums[dx, k] = dot(rows_bulk[...], w_buf[1 + k, 0 : 2 * BULK, :])
 
     def second_part(dx):
-        for core in range(2):
-            wide = x_rest[core].astype(F32)
-            rows_rest[:, core * REST : (core + 1) * REST] = (
-                wide[:, dx * CAP : (dx + 1) * CAP, :].reshape(EXPERTS * CAP, REST).astype(BF16)
-            )
-        rows = rows_rest[...]
+        rows = rows_rest[dx]
         gate = sums[dx, 0] + dot(rows, w_buf[1, 2 * BULK :, :])
         up = sums[dx, 1] + dot(rows, w_buf[2, 2 * BULK :, :])
         active = (gate / (1.0 + jnp.exp(-gate)) * up).astype(BF16)
@@ -533,33 +612,11 @@
         total = (sums[dx, 0] + y_recv[dx].astype(F32)).reshape(EXPERTS, CAP, HALF)
         parts[dx, :, 0:CAP, :] = total[:, :, 0:REST].astype(BF16)
         parts[dx, :, CAP:, :] = total[:, :, REST:BULK].astype(BF16)
-        pair, at = (0 if dx >= 2 else 1), (0 if dx in (2, 1) else CAP)
+        pair, at = (0 if dx in (1, 3) else 1), (0 if dx > 1 else CAP)
         rest_send[pair, :, at : at + CAP, :] = total[:, :, BULK:].astype(BF16)
 
     for copy in weight_copies[4:]:
         copy.wait()
-    first_part(0)
-    for i, a in enumerate(ORDER):
-        x_ring(0, 0, 3, a).wait_recv()
-        if i < 2:
-            x_ring(0, 3, 2, a).start()
-        x_twin(3, a, False).start()
-        x_ring(1, 0, 1, a).wait_recv()
-        if i >= 2:
-            x_ring(1, 1, 2, a).start()
-        x_twin(1, a, False).start()
-    first_part(3)
-    first_part(1)
-    for a in ORDER:
-        wait_group(a, disp_rest, x_rest.at[c], e_ss, e_rs)
-        rest_twin(a, False).start()
-    for i, a in enumerate(ORDER):
-        x_ring(0 if i < 2 else 1, 0, 2, a).wait_recv()
-        x_twin(2, a, False).start()
-    first_part(2)
-    for a in ORDER:
-        rest_twin(a, True).wait_recv()
-
     def half(h):
         return pl.ds(8 * h, 8)
 
@@ -577,35 +634,108 @@
             right if dx == 1 else left,
         )
 
-    def rest_back(pair, a, b):
-        return over_plane(
-            a, b, rest_send.at[pair], rest_recv.at[pair], rest_ss.at[pair], rest_rs.at[pair]
-        )
-
-    def back_copy(a, b):
-        return over_plane(a, b, back, ret, b_ss, b_rs)
+    rest_back = [
+        (rest_send.at[pair], rest_recv.at[pair], rest_ss.at[pair], rest_rs.at[pair])
+        for pair in range(2)
+    ]
+    back_way = (back, ret, b_ss, b_rs)
 
     def sum_copy(dx):
         return remote(
             sum_send.at[dx], sum_recv.at[4 - dx], sum_ss.at[dx], sum_rs.at[4 - dx], along(dx)
         )
 
-    second_part(2)
-    second_part(3)
-    settle(2)
-    far_copy(0).start()
-    far_copy(1).start()
-    settle(3)
-    near_copy(3, 0).start()
-    for a, b in FAR_FIRST:
-        rest_back(0, a, b).start()
-    second_part(1)
-    second_part(0)
-    settle(1)
-    near_copy(1, 1).start()
+    @pl.loop(0, 8)
+    def _(step):
+        def at(number):
+            return pl.when(step == number)
+
+        @at(0)
+        def _():
+            for a in GROUPS:
+                x_twin(0, a, True).wait_recv()
+
+        @at(1)
+        def _():
+            for i, a in enumerate(GROUPS):
+                x_ring(0, 0, 3, a).wait_recv()
+                if i < 2:
+                    x_ring(0, 3, 2, a).start()
+                x_twin(3, a, False).start()
+                x_ring(1, 0, 1, a).wait_recv()
+                if i >= 2:
+                    x_ring(1, 1, 2, a).start()
+                x_twin(1, a, False).start()
+            for a in GROUPS:
+                x_twin(3, a, True).wait_recv()
+
+        @at(2)
+        def _():
+            for a in GROUPS:
+                x_twin(1, a, True).wait_recv()
+
+        @at(3)
+        def _():
+            for a in ORDER:
+                wait_group(a, *rest_way)
+                rest_twin(a, False).start()
+            for a in ORDER:
+                rest_twin(a, True).wait_recv()
+            for core in range(2):
+                wide = x_rest[core].astype(F32)
+                for dx in range(4):
+                    rows_rest[dx, :, core * REST : (core + 1) * REST] = (
+                        wide[:, dx * CAP : (dx + 1) * CAP, :]
+                        .reshape(EXPERTS * CAP, REST)
+                        .astype(BF16)
+                    )
+
+        @at(4)
+        def _():
+            for i, a in enumerate(GROUPS):
+                x_ring(0 if i < 2 else 1, 0, 2, a).wait_recv()
+                x_twin(2, a, False).start()
+
+        @at(5)
+        def _():
+            for a in GROUPS:
+                x_twin(2, a, True).wait_recv()
+
+        @at(6)
+        def _():
+            settle(3)
+            near_copy(3, 0).start()
+            settle(1)
+            near_copy(1, 1).start()
+            over_plane(*rest_back[0])
+
+        @at(7)
+        def _():
+            settle(2)
+            far_copy(0).start()
+            far_copy(1).start()
+
+        is_first = jnp.logical_or(step < 3, step == 5)
+        dx = jnp.where(
+            jnp.logical_or(step == 0, step == 7),
+            0,
+            jnp.where(
+                jnp.logical_or(step == 1, step == 3),
+                3,
+                jnp.where(jnp.logical_or(step == 2, step == 4), 1, 2),
+            ),
+        )
+
+        @pl.when(is_first)
+        def _():
+            first_part(dx)
+
+        @pl.when(jnp.logical_not(is_first))
+        def _():
+            second_part(dx)
+
     settle(0)
-    for a, b in FAR_FIRST:
-        rest_back(1, a, b).start()
+    over_plane(*rest_back[1])
     far_copy(0).wait_recv()
     parts[1, 0:8] = (parts[1, 0:8].astype(F32) + diag_recv[0].astype(F32)).astype(BF16)
     near_copy(1, 0).start()
@@ -626,13 +756,13 @@
 
         both = rest_recv[pair].astype(F32)
         found = []
-        for i, dx in enumerate((2, 3) if pair == 0 else (1, 0)):
+        for i, dx in enumerate((3, 1) if pair == 0 else (2, 0)):
             table = both[:, i * CAP : (i + 1) * CAP, :].reshape(EXPERTS * CAP, REST).astype(BF16)
             found.append(combine(dx, table))
         return found
 
     found = rest_sums(0)
-    for i, dx in enumerate((2, 3)):
+    for i, dx in enumerate((3, 1)):
         sum_send[dx] = found[i].astype(BF16)
         sum_copy(dx).start()
     for h in range(2):
@@ -642,11 +772,10 @@
         back[at] = (
             parts[0, at].astype(F32) + side_recv[0, at].astype(F32) + side_recv[1, at].astype(F32)
         ).astype(BF16)
-    for a, b in FAR_FIRST:
-        back_copy(a, b).start()
+    over_plane(*back_way)
     found = rest_sums(1)
-    sum_send[1] = found[0].astype(BF16)
-    sum_copy(1).start()
+    sum_send[2] = found[0].astype(BF16)
+    sum_copy(2).start()
     rest = moe_half[2, :, BULK:] + found[1]
     for dx in (2, 1, 3):
         sum_copy(4 - dx).wait_recv()
@@ -678,17 +807,18 @@
             twin_copy(dx, h).wait_send()
     proj_copy.wait_send()
 
-    for a, b in FAR_FIRST[:15]:
-        bulk_copy(a, b).wait_send()
-        rest_copy(a, b).wait_send()
-        rest_back(0, a, b).wait_send()
-        rest_back(1, a, b).wait_send()
-        back_copy(a, b).wait_send()
+    @pl.loop(0, 16)
+    def _(p):
+        @pl.when(p != plane)
+        def _():
+            for way in (bulk_way, rest_way, rest_back[0], rest_back[1], back_way):
+                plane_gone(*way, p)
+
     for dx in (1, 2, 3):
         to_line(info, info_ss, info_rs, dx).wait_send()
         to_line(tok_rest, tok_ss, tok_rs, dx).wait_send()
         sum_copy(dx).wait_send()
-    for i, a in enumerate(ORDER):
+    for i, a in enumerate(GROUPS):
         x_ring(0, 0, 3, a).wait_send()
         x_ring(1, 0, 1, a).wait_send()
         (x_ring(0, 3, 2, a) if i < 2 else x_ring(1, 1, 2, a)).wait_send()
@@ -720,15 +850,22 @@
     pairs = (EXPERTS, 2 * CAP, REST)
     fours = (EXPERTS, 4 * CAP, REST)
     scratch = [
+        pltpu.VMEM((TOK, D), BF16),
+        pltpu.VMEM((D,), F32),
+        pltpu.VMEM((D,), F32),
+        pltpu.VMEM((2, TOK), jnp.int32),
+        pltpu.VMEM((2, TOK), F32),
+        dma((5,)),
         pltpu.VMEM((3, D, HALF), BF16),
         pltpu.VMEM((HALF, D), BF16),
         pltpu.VMEM((2, HALF, HALF), BF16),
         dma((14,)),
-        pltpu.VMEM((2, 8, HD, TOK), BF16),
-        pltpu.VMEM((8, HD, TOK), BF16),
-        pltpu.VMEM((TOK, 8 * TOK), BF16),
+        pltpu.VMEM((TOK, D), BF16),
+        pltpu.VMEM((3, 8, HD, TOK), BF16),
+        pltpu.VMEM((HD, 8 * TOK), BF16),
         pltpu.VMEM((8, 2 * HD + 32, 8 * TOK), BF16),
-        pltpu.VMEM((8 * TOK, TOK), BF16),
+        pltpu.VMEM((8 * TOK, 8 * TOK), F32),
+        pltpu.VMEM((1, 8 * TOK), F32),
         pltpu.VMEM((1, 8 * TOK), F32),
         pltpu.VMEM((TOK, 8 * TOK), F32),
         pltpu.VMEM((8, HD, TOK), BF16),
@@ -737,6 +874,9 @@
         pltpu.VMEM((TOK, D), BF16),
         pltpu.VMEM((3, TOK, HALF), F32),
         pltpu.VMEM((4, 8, TOK), F32),
+        pltpu.VMEM((4, EXPERTS * CAP, TOK), BF16),
+        pltpu.VMEM((4, 2 * TOK, EXPERTS * CAP), BF16),
+        pltpu.VMEM((4, 2, TOK, TOK), F32),
         pltpu.VMEM((4, TOK, REST), BF16),
         pltpu.VMEM(pairs, BF16),
         pltpu.VMEM(fours, F32),
@@ -744,7 +884,7 @@
         pltpu.VMEM((4, 2) + pairs, BF16),
         pltpu.VMEM((2,) + fours, BF16),
         pltpu.VMEM((EXPERTS * CAP, 2 * BULK), BF16),
-        pltpu.VMEM((EXPERTS * CAP, 2 * REST), BF16),
+        pltpu.VMEM((4, EXPERTS * CAP, 2 * REST), BF16),
         pltpu.VMEM((4, 2, EXPERTS * CAP, HALF), F32),
         pltpu.VMEM((4, EXPERTS * CAP, HALF), BF16),
         pltpu.VMEM((4, EXPERTS * CAP, HALF), BF16),
@@ -796,7 +936,7 @@
     return pl.pallas_call(
         layer_kernel,
         out_shape=jax.ShapeDtypeStruct((TOK, HALF), BF16),
-        in_specs=[vmem, hbm, hbm, vmem, vmem, vmem, vmem, hbm, hbm],
+        in_specs=[hbm] * 9,
         out_specs=vmem,
         scratch_shapes=scratch,
         compiler_params=pltpu.CompilerParams(

time: 103 us -> 98.9 us (0.960)
  Pallas kernels: 101 us -> 97.2 us
    pallas_call x1, Pallas kernels: 101 us -> 97.2 us  [on_device(): pl.pallas_call(layer_kernel, out_shape=jax.ShapeDtypeStruct((TOK, HALF),...]
where the time goes in v3:
time: 98.9 us; the launch traced here: 98.8 us
  Pallas kernels  97.2 us (98%)
  local copies, waits for them, and re-layouts  1.62 us (2%)
    pallas_call x1, Pallas kernels, on_device(): pl.pallas_call(layer_kernel, out_shape=jax.ShapeDtypeStruct((TOK, HALF),...  97.2 us

profile of v3, /device:TPU:0, one launch (start us, length us, event | category | flops | bytes accessed | tf_op | source)
XLA Modules:
  0.0 98.8 jit_solution(13748525119542384425)
XLA Ops:
  0.0 97.2 %shard_map.91 = bf16[128,768]{1,0:T(8,128)(2,1)} custom-call(bf16[128,1536]{1,0:T(8,128)(2,1)} %tokens_in.1, bf16[3,1536,768]{2,1,0:T(8,128)(2,1)} %attn_w.1, bf16[768,1536]{1,0:T(8,128)(2,1)} %out_w.1, f32[1536]{0:T(1024)} %norm_attn_in.1, f32[1536]{0:T(1024)} %norm_moe_in.1, s32[2,128]{1,0:T(2,128)} %bitcast.2, f32[2,128]{1,0:T(2,128)} %bitcast.3, ...), custom_call_target="tpu_custom_call" | custom-call | flops 30000001024 | bytes 17000000 | tf_op jit(solution)/shard_map/pallas_call | solution.py:936
  97.2 1.6 %copy.11 = bf16[128,768]{1,0:T(8,128)(2,1)} copy(bf16[128,768]{1,0:T(8,128)(2,1)} %shard_map.91) | data formatting | bytes 393216

commit v4 on v3

--- a/solution.py
+++ b/solution.py
@@ -510,6 +510,17 @@
     disp_bulk[:, 0:CAP, :] = rows[:, :, 0:REST].astype(BF16)
     disp_bulk[:, CAP:, :] = rows[:, :, REST:].astype(BF16)
 
+    def to_plane(p, src, dst, send_sem, recv_sem):
+        @pl.when(p == plane)
+        def _():
+            pltpu.make_async_copy(src.at[p], dst.at[plane], recv_sem.at[plane]).start()
+
+        @pl.when(p != plane)
+        def _():
+            remote(
+                src.at[p], dst.at[plane], send_sem.at[p], recv_sem.at[plane], plane_dev(p)
+            ).start()
+
     def over_plane(src, dst, send_sem, recv_sem, near=False):
         @pl.loop(0, 16)
         def _(i):
@@ -519,16 +530,7 @@
             else:
                 a = (2 + 3 * turn) % 4
             p = ((z + a) % 4) * 4 + (y + 2 + 3 * i) % 4
-
-            @pl.when(p == plane)
-            def _():
-                pltpu.make_async_copy(src.at[p], dst.at[plane], recv_sem.at[plane]).start()
-
-            @pl.when(p != plane)
-            def _():
-                remote(
-                    src.at[p], dst.at[plane], send_sem.at[p], recv_sem.at[plane], plane_dev(p)
-                ).start()
+            to_plane(p, src, dst, send_sem, recv_sem)
 
     def plane_gone(src, dst, send_sem, recv_sem, p):
         remote(src.at[p], dst.at[plane], send_sem.at[p], recv_sem.at[plane], plane_dev(p)).wait_send()
@@ -617,20 +619,25 @@
 
     for copy in weight_copies[4:]:
         copy.wait()
-    def half(h):
-        return pl.ds(8 * h, 8)
-
-    def far_copy(h):
+    def piece_of(h, q):
+        return pl.ds(8 * h + 4 * q, 4)
+
+    def far_copy(h, q):
         return remote(
-            parts.at[2, half(h)], diag_recv.at[h], r_ss.at[h], r_rs.at[h], right if h == 0 else left
-        )
-
-    def near_copy(dx, h):
+            parts.at[2, piece_of(h, q)],
+            diag_recv.at[h, pl.ds(4 * q, 4)],
+            r_ss.at[h, q],
+            r_rs.at[h, q],
+            right if h == 0 else left,
+        )
+
+    def near_copy(dx, h, q):
+        number = 2 + (dx // 2) * 2 + h
         return remote(
-            parts.at[dx, half(h)],
-            side_recv.at[dx // 2, half(h)],
-            r_ss.at[2 + (dx // 2) * 2 + h],
-            r_rs.at[2 + (dx // 2) * 2 + h],
+            parts.at[dx, piece_of(h, q)],
+            side_recv.at[dx // 2, piece_of(h, q)],
+            r_ss.at[number, q],
+            r_rs.at[number, q],
             right if dx == 1 else left,
         )
 
@@ -704,16 +711,19 @@
         @at(6)
         def _():
             settle(3)
-            near_copy(3, 0).start()
+            for q in range(2):
+                near_copy(3, 0, q).start()
             settle(1)
-            near_copy(1, 1).start()
+            for q in range(2):
+                near_copy(1, 1, q).start()
             over_plane(*rest_back[0])
 
         @at(7)
         def _():
             settle(2)
-            far_copy(0).start()
-            far_copy(1).start()
+            for q in range(2):
+                far_copy(0, q).start()
+                far_copy(1, q).start()
 
         is_first = jnp.logical_or(step < 3, step == 5)
         dx = jnp.where(
@@ -736,12 +746,13 @@
 
     settle(0)
     over_plane(*rest_back[1])
-    far_copy(0).wait_recv()
-    parts[1, 0:8] = (parts[1, 0:8].astype(F32) + diag_recv[0].astype(F32)).astype(BF16)
-    near_copy(1, 0).start()
-    far_copy(1).wait_recv()
-    parts[3, 8:16] = (parts[3, 8:16].astype(F32) + diag_recv[1].astype(F32)).astype(BF16)
-    near_copy(3, 1).start()
+    for q in range(2):
+        for h, dx in ((0, 1), (1, 3)):
+            far_copy(h, q).wait_recv()
+            at = slice(8 * h + 4 * q, 8 * h + 4 * q + 4)
+            far_part = diag_recv[h, 4 * q : 4 * q + 4].astype(F32)
+            parts[dx, at] = (parts[dx, at].astype(F32) + far_part).astype(BF16)
+            near_copy(dx, h, q).start()
 
     def rest_sums(pair):
         @pl.loop(0, 16)
@@ -765,14 +776,18 @@
     for i, dx in enumerate((3, 1)):
         sum_send[dx] = found[i].astype(BF16)
         sum_copy(dx).start()
-    for h in range(2):
-        near_copy(1, h).wait_recv()
-        near_copy(3, h).wait_recv()
-        at = slice(8 * h, 8 * h + 8)
-        back[at] = (
-            parts[0, at].astype(F32) + side_recv[0, at].astype(F32) + side_recv[1, at].astype(F32)
-        ).astype(BF16)
-    over_plane(*back_way)
+    for q in range(2):
+        for h in range(2):
+            near_copy(1, h, q).wait_recv()
+            near_copy(3, h, q).wait_recv()
+            at = slice(8 * h + 4 * q, 8 * h + 4 * q + 4)
+            near_parts = side_recv[0, at].astype(F32) + side_recv[1, at].astype(F32)
+            back[at] = (parts[0, at].astype(F32) + near_parts).astype(BF16)
+
+        @pl.loop(0, 8)
+        def _(i):
+            to_plane(2 * 4 * far(i) + 4 * q + (y + 2 + 3 * (i // 2)) % 4, *back_way)
+
     found = rest_sums(1)
     sum_send[2] = found[0].astype(BF16)
     sum_copy(2).start()
@@ -828,9 +843,10 @@
     for dx in range(4):
         y_copy(dx).wait_send()
     for h in range(2):
-        far_copy(h).wait_send()
-        near_copy(1, h).wait_send()
-        near_copy(3, h).wait_send()
+        for q in range(2):
+            far_copy(h, q).wait_send()
+            near_copy(1, h, q).wait_send()
+            near_copy(3, h, q).wait_send()
 
 
 def on_device(
@@ -924,8 +940,8 @@
         dma((4,)),
         dma((4,)),
         dma((4,)),
-        dma((6,)),
-        dma((6,)),
+        dma((6, 2)),
+        dma((6, 2)),
         dma((2, 16)),
         dma((2, 16)),
         dma((4,)),

time: 98.9 us -> 95.7 us (0.968)
  Pallas kernels: 97.2 us -> 94 us
    pallas_call x1, Pallas kernels: 97.2 us -> 94 us  [on_device(): pl.pallas_call(layer_kernel, out_shape=jax.ShapeDtypeStruct((TOK, HALF),...]
where the time goes in v4:
time: 95.7 us; the launch traced here: 95.6 us
  Pallas kernels  94 us (98%)
  local copies, waits for them, and re-layouts  1.62 us (2%)
    pallas_call x1, Pallas kernels, on_device(): pl.pallas_call(layer_kernel, out_shape=jax.ShapeDtypeStruct((TOK, HALF),...  94 us

profile of v4, /device:TPU:0, one launch (start us, length us, event | category | flops | bytes accessed | tf_op | source)
XLA Modules:
  0.0 95.6 jit_solution(8592120583030073349)
XLA Ops:
  0.0 94.0 %shard_map.91 = bf16[128,768]{1,0:T(8,128)(2,1)} custom-call(bf16[128,1536]{1,0:T(8,128)(2,1)} %tokens_in.1, bf16[3,1536,768]{2,1,0:T(8,128)(2,1)} %attn_w.1, bf16[768,1536]{1,0:T(8,128)(2,1)} %out_w.1, f32[1536]{0:T(1024)} %norm_attn_in.1, f32[1536]{0:T(1024)} %norm_moe_in.1, s32[2,128]{1,0:T(2,128)} %bitcast.2, f32[2,128]{1,0:T(2,128)} %bitcast.3, ...), custom_call_target="tpu_custom_call" | custom-call | flops 30000001024 | bytes 17000000 | tf_op jit(solution)/shard_map/pallas_call | solution.py:952
  94.0 1.6 %copy.11 = bf16[128,768]{1,0:T(8,128)(2,1)} copy(bf16[128,768]{1,0:T(8,128)(2,1)} %shard_map.91) | data formatting | bytes 393216

commit v5 on v4

--- a/solution.py
+++ b/solution.py
@@ -772,10 +772,6 @@
             found.append(combine(dx, table))
         return found
 
-    found = rest_sums(0)
-    for i, dx in enumerate((3, 1)):
-        sum_send[dx] = found[i].astype(BF16)
-        sum_copy(dx).start()
     for q in range(2):
         for h in range(2):
             near_copy(1, h, q).wait_recv()
@@ -787,6 +783,12 @@
         @pl.loop(0, 8)
         def _(i):
             to_plane(2 * 4 * far(i) + 4 * q + (y + 2 + 3 * (i // 2)) % 4, *back_way)
+
+        if q == 0:
+            found = rest_sums(0)
+            for i, dx in enumerate((3, 1)):
+                sum_send[dx] = found[i].astype(BF16)
+                sum_copy(dx).start()
 
     found = rest_sums(1)
     sum_send[2] = found[0].astype(BF16)

time: 95.7 us -> 95 us (level)
  no operation moved by 1% of the time
where the time goes in v5:
time: 95 us; the launch traced here: 94.9 us
  Pallas kernels  93.3 us (98%)
  local copies, waits for them, and re-layouts  1.62 us (2%)
    pallas_call x1, Pallas kernels, on_device(): pl.pallas_call(layer_kernel, out_shape=jax.ShapeDtypeStruct((TOK, HALF),...  93.3 us

profile of v5, /device:TPU:0, one launch (start us, length us, event | category | flops | bytes accessed | tf_op | source)
XLA Modules:
  0.0 94.9 jit_solution(17516080495989478137)
XLA Ops:
  0.0 93.3 %shard_map.91 = bf16[128,768]{1,0:T(8,128)(2,1)} custom-call(bf16[128,1536]{1,0:T(8,128)(2,1)} %tokens_in.1, bf16[3,1536,768]{2,1,0:T(8,128)(2,1)} %attn_w.1, bf16[768,1536]{1,0:T(8,128)(2,1)} %out_w.1, f32[1536]{0:T(1024)} %norm_attn_in.1, f32[1536]{0:T(1024)} %norm_moe_in.1, s32[2,128]{1,0:T(2,128)} %bitcast.2, f32[2,128]{1,0:T(2,128)} %bitcast.3, ...), custom_call_target="tpu_custom_call" | custom-call | flops 30000001024 | bytes 17000000 | tf_op jit(solution)/shard_map/pallas_call | solution.py:954
  93.3 1.6 %copy.11 = bf16[128,768]{1,0:T(8,128)(2,1)} copy(bf16[128,768]{1,0:T(8,128)(2,1)} %shard_map.91) | data formatting | bytes 393216

commit v6 on v5

--- a/solution.py
+++ b/solution.py
@@ -315,21 +315,28 @@
     def kv_part(dx, dc, h):
         return kvb.at[2 * dx + dc, pl.ds(h * HD, HD)]
 
-    def ring_copy(to, src_dx, dst_dx, h):
-        device = right if to == 0 else left
+    def ring_part(dx, h, part):
+        if part is None:
+            return kv_part(dx, 0, h)
+        return kvb.at[2 * dx, pl.ds(h * HD, HD), pl.ds(part * 4 * TOK, 4 * TOK)]
+
+    def ring_copy(to, src_dx, dst_dx, h, part=None):
         return remote(
-            kv_part(src_dx, 0, h),
-            kv_part(dst_dx, 0, h),
-            ring_ss.at[dst_dx, h],
-            ring_rs.at[dst_dx, h],
-            device,
+            ring_part(src_dx, h, part),
+            ring_part(dst_dx, h, part),
+            ring_ss.at[dst_dx, h, part or 0],
+            ring_rs.at[dst_dx, h, part or 0],
+            right if to == 0 else left,
         )
 
     def twin_copy(dx, h):
         return remote(kv_part(dx, 0, h), kv_part(dx, 1, h), twin_ss.at[dx, h], twin_rs.at[dx, h], twin)
 
-    ring_own = [[ring_copy(0, 0, 3, h), ring_copy(1, 0, 1, h)] for h in range(2)]
-    ring_on = [ring_copy(0, 3, 2, 0), ring_copy(1, 1, 2, 1)]
+    ring_own = [
+        [[ring_copy(0, 0, 3, 0)], [ring_copy(1, 0, 1, 0)]],
+        [[ring_copy(0, 0, 3, 1)], [ring_copy(1, 0, 1, 1, part) for part in range(2)]],
+    ]
+    ring_on = [[ring_copy(0, 3, 2, 0)], [ring_copy(1, 1, 2, 1, part) for part in range(2)]]
     for h in range(2):
 
         @pl.loop(0, 8)
@@ -342,8 +349,8 @@
                 mate(i),
             ).wait_recv()
 
-        ring_own[h][0].start()
-        ring_own[h][1].start()
+        for copy in ring_own[h][0] + ring_own[h][1]:
+            copy.start()
         twin_copy(0, h).start()
 
     @pl.loop(0, 8)
@@ -395,19 +402,20 @@
 
         @pl.when(step == 2)
         def _():
-            ring_own[0][0].wait_recv()
-            ring_on[0].start()
+            ring_own[0][0][0].wait_recv()
+            ring_on[0][0].start()
             twin_copy(3, 0).start()
-            ring_own[0][1].wait_recv()
+            ring_own[0][1][0].wait_recv()
             twin_copy(1, 0).start()
             twin_copy(0, 1).wait_recv()
 
         @pl.when(step == 3)
         def _():
-            ring_own[1][1].wait_recv()
-            ring_on[1].start()
+            for part in range(2):
+                ring_own[1][1][part].wait_recv()
+                ring_on[1][part].start()
             twin_copy(1, 1).start()
-            ring_own[1][0].wait_recv()
+            ring_own[1][0][0].wait_recv()
             twin_copy(3, 1).start()
 
         @pl.when(step == 4)
@@ -421,13 +429,14 @@
 
         @pl.when(step == 6)
         def _():
-            ring_on[0].wait_recv()
+            ring_on[0][0].wait_recv()
             twin_copy(2, 0).start()
             twin_copy(1, 1).wait_recv()
 
         @pl.when(step == 7)
         def _():
-            ring_on[1].wait_recv()
+            for copy in ring_on[1]:
+                copy.wait_recv()
             twin_copy(2, 1).start()
             twin_copy(2, 0).wait_recv()
 
@@ -705,14 +714,14 @@
 
         @at(5)
         def _():
-            for a in GROUPS:
-                x_twin(2, a, True).wait_recv()
-
-        @at(6)
-        def _():
             settle(3)
             for q in range(2):
                 near_copy(3, 0, q).start()
+            for a in GROUPS:
+                x_twin(2, a, True).wait_recv()
+
+        @at(6)
+        def _():
             settle(1)
             for q in range(2):
                 near_copy(1, 1, q).start()
@@ -817,9 +826,8 @@
         o_copy(i, False)
 
     for h in range(2):
-        ring_own[h][0].wait_send()
-        ring_own[h][1].wait_send()
-        ring_on[h].wait_send()
+        for copy in ring_own[h][0] + ring_own[h][1] + ring_on[h]:
+            copy.wait_send()
         for dx in range(4):
             twin_copy(dx, h).wait_send()
     proj_copy.wait_send()
@@ -919,8 +927,8 @@
         dma((2, 8)),
         dma((8,)),
         dma((8,)),
-        dma((4, 2)),
-        dma((4, 2)),
+        dma((4, 2, 2)),
+        dma((4, 2, 2)),
         dma((4, 2)),
         dma((4, 2)),
         dma((8,)),

time: 95 us -> 94.7 us (level)
  no operation moved by 1% of the time
where the time goes in v6:
time: 94.7 us; the launch traced here: 94.6 us
  Pallas kernels  93 us (98%)
  local copies, waits for them, and re-layouts  1.62 us (2%)
    pallas_call x1, Pallas kernels, on_device(): pl.pallas_call(layer_kernel, out_shape=jax.ShapeDtypeStruct((TOK, HALF),...  93 us

profile of v6, /device:TPU:0, one launch (start us, length us, event | category | flops | bytes accessed | tf_op | source)
XLA Modules:
  0.0 94.6 jit_solution(11259861978812153075)
XLA Ops:
  0.0 93.0 %shard_map.91 = bf16[128,768]{1,0:T(8,128)(2,1)} custom-call(bf16[128,1536]{1,0:T(8,128)(2,1)} %tokens_in.1, bf16[3,1536,768]{2,1,0:T(8,128)(2,1)} %attn_w.1, bf16[768,1536]{1,0:T(8,128)(2,1)} %out_w.1, f32[1536]{0:T(1024)} %norm_attn_in.1, f32[1536]{0:T(1024)} %norm_moe_in.1, s32[2,128]{1,0:T(2,128)} %bitcast.2, f32[2,128]{1,0:T(2,128)} %bitcast.3, ...), custom_call_target="tpu_custom_call" | custom-call | flops 30000001024 | bytes 17000000 | tf_op jit(solution)/shard_map/pallas_call | solution.py:962
  93.0 1.6 %copy.11 = bf16[128,768]{1,0:T(8,128)(2,1)} copy(bf16[128,768]{1,0:T(8,128)(2,1)} %shard_map.91) | data formatting | bytes 393216

commit v7 on v6

--- a/solution.py
+++ b/solution.py
@@ -725,10 +725,10 @@
             settle(1)
             for q in range(2):
                 near_copy(1, 1, q).start()
+
+        @at(7)
+        def _():
             over_plane(*rest_back[0])
-
-        @at(7)
-        def _():
             settle(2)
             for q in range(2):
                 far_copy(0, q).start()

time: 94.7 us -> 94.5 us (level)
  no operation moved by 1% of the time
where the time goes in v7:
time: 94.5 us; the launch traced here: 94.3 us
  Pallas kernels  92.7 us (98%)
  local copies, waits for them, and re-layouts  1.62 us (2%)
    pallas_call x1, Pallas kernels, on_device(): pl.pallas_call(layer_kernel, out_shape=jax.ShapeDtypeStruct((TOK, HALF),...  92.7 us

profile of v7, /device:TPU:0, one launch (start us, length us, event | category | flops | bytes accessed | tf_op | source)
XLA Modules:
  0.0 94.3 jit_solution(17940758688102566404)
XLA Ops:
  0.0 92.7 %shard_map.91 = bf16[128,768]{1,0:T(8,128)(2,1)} custom-call(bf16[128,1536]{1,0:T(8,128)(2,1)} %tokens_in.1, bf16[3,1536,768]{2,1,0:T(8,128)(2,1)} %attn_w.1, bf16[768,1536]{1,0:T(8,128)(2,1)} %out_w.1, f32[1536]{0:T(1024)} %norm_attn_in.1, f32[1536]{0:T(1024)} %norm_moe_in.1, s32[2,128]{1,0:T(2,128)} %bitcast.2, f32[2,128]{1,0:T(2,128)} %bitcast.3, ...), custom_call_target="tpu_custom_call" | custom-call | flops 30000001024 | bytes 17000000 | tf_op jit(solution)/shard_map/pallas_call | solution.py:962
  92.7 1.6 %copy.11 = bf16[128,768]{1,0:T(8,128)(2,1)} copy(bf16[128,768]{1,0:T(8,128)(2,1)} %shard_map.91) | data formatting | bytes 393216
